TPU v7x, 32 devices: a whole 2x2x4 slice. The times are simulated.
32 devices in a mesh: date: 8 (over z, x), row: 2 (over core), col: 2 (over y).
Axes of the slice: x: 2, y: 2, z: 4, core: 2. Of those that a mesh axis runs over, the one named last changes fastest.
Arguments:
- images: float32 [16, 2, 96, 1536], P('date', None, 'row', 'col'), may hold values from -8 to 8
- secondaries: int32 [16, 3], P('date'), may hold values from 0 to 15, as said below
Outputs:
- filtered: float32 [16, 3, 2, 48, 192], P('date', None, None, 'row', 'col')
- coherence: float32 [16, 3, 2, 48, 192], P('date', None, None, 'row', 'col')
Inputs may be any that keep to these rules, and one draw needn't show every extreme that they name: secondaries[k, l] = (k + o) mod 16 for 3 distinct offsets o of 1 to 4, rising with l; the offset 4 occurs in every draw.
All inputs are finite; a program needn't handle non-finite values.
Results may differ from a plain program's by a relative error of at most 0.00005.
Values sent between devices are 32-bit elements; how exact they have to be, the bound alone decides.
A program may use at most 128 MiB of HBM per device.

v0:
```python
import math

import jax
import jax.numpy as jnp
from jax import lax
from jax.sharding import PartitionSpec as P

LOOK_R = 2
LOOK_C = 8
PATCH = 32
KEEP = 24
MARGIN = 4


def shifted(value, axis, steps):
    count = lax.axis_size(axis)
    pairs = [(source, (source + steps) % count) for source in range(count)]
    return lax.ppermute(value, axis, pairs)


def with_halo(block, sides, width):
    for axis, dim in sides:
        count = lax.axis_size(axis)
        forward = [(i, i + 1) for i in range(count - 1)]
        backward = [(target, source) for source, target in forward]
        low = lax.ppermute(
            lax.slice_in_dim(block, block.shape[dim] - width, None, axis=dim), axis, forward
        )
        high = lax.ppermute(lax.slice_in_dim(block, 0, width, axis=dim), axis, backward)
        block = jnp.concatenate([low, block, high], axis=dim)
    return block


def multilook(values):
    extent = values.shape
    blocks = values.reshape(
        extent[:-2] + (extent[-2] // LOOK_R, LOOK_R, extent[-1] // LOOK_C, LOOK_C)
    )
    return blocks.mean(axis=(-3, -1))


def window_last(grid_values, block_count):
    leading = grid_values.shape[:-1]
    head_part = grid_values[..., : block_count * KEEP].reshape(leading + (block_count, KEEP))
    widths = [(0, 0)] * (grid_values.ndim - 1) + [(0, 2 * KEEP - PATCH)]
    extended = jnp.pad(grid_values, widths)
    tail_part = extended[..., KEEP:].reshape(leading + (block_count, KEEP))[..., : PATCH - KEEP]
    return jnp.concatenate([head_part, tail_part], axis=-1)


def patches(grid_values, row_blocks, col_blocks):
    across = window_last(grid_values, col_blocks)
    turned = jnp.moveaxis(across, -3, -1)
    stacked = window_last(turned, row_blocks)
    return jnp.moveaxis(stacked, (-4, -3), (-2, -1))


def box_mean(padded, rows_out, cols_out):
    summed = jnp.zeros(padded.shape[:-2] + (rows_out, cols_out), padded.dtype)
    for row_step in (-1, 0, 1):
        for col_step in (-1, 0, 1):
            summed = (
                summed
                + padded[
                    ...,
                    MARGIN + row_step : MARGIN + row_step + rows_out,
                    MARGIN + col_step : MARGIN + col_step + cols_out,
                ]
            )
    return summed / 9.0


def coherence_from(real_pad, imag_pad, first_pad, second_pad, rows_out, cols_out):
    cross_real = box_mean(real_pad, rows_out, cols_out)
    cross_imag = box_mean(imag_pad, rows_out, cols_out)
    energy = box_mean(first_pad, rows_out, cols_out) * box_mean(second_pad, rows_out, cols_out)
    factor = lax.rsqrt(energy + 1e-06)
    return jnp.stack([cross_real * factor, cross_imag * factor], axis=-3)


def weights_of(power):
    smooth = jnp.zeros_like(power)
    for row_step in (-1, 0, 1):
        for col_step in (-1, 0, 1):
            smooth = smooth + jnp.roll(power, (row_step, col_step), axis=(-3, -1))
    smooth = smooth / 9.0
    level = jnp.mean(power, axis=(-3, -1), keepdims=True)
    weight = (smooth + level + 1e-06) ** 0.25
    return weight / jnp.mean(weight, axis=(-3, -1), keepdims=True)


def centre(values, row_blocks, col_blocks):
    kept = values[..., MARGIN : MARGIN + KEEP, :, MARGIN : MARGIN + KEEP]
    return kept.reshape(kept.shape[:-4] + (row_blocks * KEEP, col_blocks * KEEP))


def spectral(real_part, imag_part, sign):
    ticks = jnp.arange(PATCH, dtype=jnp.int32)
    angle = (ticks[:, None] * ticks[None, :] % PATCH).astype(jnp.float32) * (2.0 * math.pi / PATCH)
    cosine = jnp.cos(angle)
    sine = sign * jnp.sin(angle)
    highest = lax.Precision.HIGHEST

    def along_rows(table, values):
        return jnp.einsum("uy,...ybx->...ubx", table, values, precision=highest)

    def along_cols(table, values):
        return jnp.einsum("vx,...ybx->...ybv", table, values, precision=highest)

    middle_real = along_rows(cosine, real_part) - along_rows(sine, imag_part)
    middle_imag = along_rows(cosine, imag_part) + along_rows(sine, real_part)
    final_real = along_cols(cosine, middle_real) - along_cols(sine, middle_imag)
    final_imag = along_cols(cosine, middle_imag) + along_cols(sine, middle_real)
    return (final_real, final_imag)


def goldstein(real_pad, imag_pad, row_blocks, col_blocks):
    real_part = patches(real_pad, row_blocks, col_blocks)
    imag_part = patches(imag_pad, row_blocks, col_blocks)
    spec_real, spec_imag = spectral(real_part, imag_part, -1.0)
    weight = weights_of(spec_real * spec_real + spec_imag * spec_imag)
    back_real, back_imag = spectral(spec_real * weight, spec_imag * weight, 1.0)
    scale = 1.0 / (PATCH * PATCH)
    return jnp.stack(
        [
            centre(back_real * scale, row_blocks, col_blocks),
            centre(back_imag * scale, row_blocks, col_blocks),
        ],
        axis=-3,
    )


def body(images, secondaries):
    per_device = images.shape[0]
    links = secondaries.shape[1]
    tile_rows = images.shape[2]
    tile_cols = images.shape[3]
    look_rows = tile_rows // LOOK_R
    look_cols = tile_cols // LOOK_C
    first_date = lax.axis_index("date") * per_device
    total_dates = per_device * lax.axis_size("date")
    slots = (secondaries - first_date) % total_dates
    own_date = images[:, None]
    following = shifted(images, "date", -1)
    beyond = shifted(following, "date", -1)
    window = jnp.concatenate([images, following, beyond], axis=0)
    partners = jnp.take(window, slots.reshape(-1), axis=0).reshape(
        (per_device, links) + images.shape[1:]
    )
    pair_real = multilook(
        own_date[:, :, 0] * partners[:, :, 0] + own_date[:, :, 1] * partners[:, :, 1]
    )
    pair_imag = multilook(
        own_date[:, :, 1] * partners[:, :, 0] - own_date[:, :, 0] * partners[:, :, 1]
    )
    powers = multilook(window[:, 0] * window[:, 0] + window[:, 1] * window[:, 1])
    first_power = jnp.broadcast_to(
        powers[:per_device, None], (per_device, links, look_rows, look_cols)
    )
    second_power = jnp.take(powers, slots.reshape(-1), axis=0).reshape(
        per_device, links, look_rows, look_cols
    )
    planes = jnp.stack([pair_real, pair_imag, first_power, second_power], axis=2)
    padded = with_halo(planes, (("row", 3), ("col", 4)), MARGIN)
    real_pad = padded[:, :, 0]
    imag_pad = padded[:, :, 1]
    first_pad = padded[:, :, 2]
    second_pad = padded[:, :, 3]
    coherent = coherence_from(real_pad, imag_pad, first_pad, second_pad, look_rows, look_cols)
    filtered = goldstein(real_pad, imag_pad, look_rows // KEEP, look_cols // KEEP)
    return (filtered, coherent)


def solution(mesh):
    in_specs = (P("date", None, "row", "col"), P("date", None))
    out_specs = (P("date", None, None, "row", "col"), P("date", None, None, "row", "col"))
    return jax.shard_map(body, mesh=mesh, in_specs=in_specs, out_specs=out_specs, check_vma=False)
```

profile of v0, /device:TPU:30, one launch (start us, length us, event | category | flops | bytes accessed | tf_op | source)
XLA Modules:
  0.0 130.4 jit_solution(12199991131577174891)
XLA Ops:
  2.0 1.1 fusion.184
  3.1 4.0 %mul.270 = f32[2,24,2,96,8]{4,3,2,1,0:T(8,128)} reshape(f32[2,1,1,48,768]{4,3,2,0,1:T(8,128)S(1)} %get-tuple-element.17) | data formatting | bytes 589824 | tf_op jit(solution)/shard_map/mul | solution.py:151
  7.1 4.0 %mul.266 = f32[2,24,2,96,8]{4,3,2,1,0:T(8,128)} reshape(f32[2,1,1,48,768]{4,3,2,0,1:T(8,128)S(1)} %get-tuple-element.16) | data formatting | bytes 589824 | tf_op jit(solution)/shard_map/mul | solution.py:151
  11.1 7.5 %collective-permute-done = f32[2,2,48,768]{3,2,1,0:T(8,128)S(1)} collective-permute-done((f32[2,2,48,768]{3,2,1,0:T(8,128)}, f32[2,2,48,768]{3,2,1,0:T(8,128)S(1)}, u32[]{:S(2)}, u32[]{:S(2)}) %collective-permute-start) | collective-permute-done | bytes 589856 | tf_op jit(solution)/shard_map/ppermute | solution.py:18
  18.8 16.8 %collective-permute-done.1 = f32[2,2,48,768]{3,2,1,0:T(8,128)S(1)} collective-permute-done((f32[2,2,48,768]{3,2,1,0:T(8,128)S(1)}, f32[2,2,48,768]{3,2,1,0:T(8,128)S(1)}, u32[]{:S(2)}, u32[]{:S(2)}) %collective-permute-start.1) | collective-permute-done | bytes 589856 | tf_op jit(solution)/shard_map/ppermute | solution.py:18
  35.7 9.5 %add.276 = f32[6,24,2,96,8]{4,3,2,1,0:T(8,128)} reshape(f32[6,1,48,768]{3,2,1,0:T(8,128)S(1)} %fusion.8) | data formatting | bytes 1769472 | tf_op jit(solution)/shard_map/add | solution.py:156
  45.2 7.5 %reduce_sum.47 = f32[6,24,96]{2,1,0:T(8,128)S(1)} reduce(f32[6,24,2,96,8]{4,3,2,1,0:T(8,128)} %add.276, f32[]{:T(128)} %constant.89.clone.1), dimensions={2,4}, to_apply=%region_2.3 | reduce | flops 207360 | bytes 940036 | tf_op jit(solution)/shard_map/reduce_sum | solution.py:39
  53.4 1.2 gather_fusion.1
  55.2 1.6 %broadcast_select_fusion = f32[2,3,1,24,96]{4,3,1,0,2:T(8,128)} fusion(f32[2,3,1,24,96]{4,3,1,0,2:T(8,128)} %bitcast.216, pred[2,3]{1,0:T(4,128)(4,1)S(1)} %get-tuple-element.12), kind=kLoop, calls=%fused_computation.139 | loop fusion | flops 13824 | bytes 110598 | tf_op jit(solution)/shard_map/jit(_take)/select_n | solution.py:160
  57.2 9.5 %squeeze.13 = f32[2,3,24,2,96,8]{5,4,3,2,1,0:T(8,128)} reshape(f32[2,3,1,48,768]{4,3,1,0,2:T(8,128)S(1)} %get-tuple-element.15) | data formatting | bytes 1769472 | tf_op jit(solution)/shard_map/squeeze | solution.py:151
  66.7 9.4 %squeeze.12 = f32[2,3,24,2,96,8]{5,4,3,2,1,0:T(8,128)} reshape(f32[2,3,1,48,768]{4,3,1,0,2:T(8,128)S(1)} %get-tuple-element.14) | data formatting | bytes 1769472 | tf_op jit(solution)/shard_map/squeeze | solution.py:151
  76.1 13.6 %add_reduce_fusion = (f32[2,3,24,96]{3,2,1,0:T(8,128)S(1)}, f32[2,3,24,96]{3,2,1,0:T(8,128)S(1)}) fusion(f32[2,3,24,2,96,8]{5,4,3,2,1,0:T(8,128)} %squeeze.13, f32[2,3,24,2,96,8]{5,4,3,2,1,0:T(8,128)} %squeeze.12, f32[2,24,2,96,8]{4,3,2,1,0:T(8,128)} %mul.270, f32[2,24,2,96,8]{4,3,2,1,0:T(8,128)} %mul.266), kind=kLoop, calls=%fused_computation.3 | loop fusion | flops 1741824 | bytes 2469888 | tf_op jit(solution)/shard_map/reduce_sum | solution.py:39
  89.9 1.3 collective-permute-start.3
  91.2 3.0 %collective-permute-start.2 = (f32[2,3,4,4,96]{4,3,1,0,2:T(4,128)S(1)}, f32[2,3,4,4,96]{4,3,1,0,2:T(4,128)S(1)}, u32[]{:S(2)}, u32[]{:S(2)}) collective-permute-start(f32[2,3,4,4,96]{4,3,1,0,2:T(4,128)S(1)} %get-tuple-element.48), channel_id=1, source_target_pairs={{0,2},{1,3},{4,6},{5,7},{8,10},{9,11},{12,14},{13,15},{16,18},{17,... | collective-permute-start | bytes 110600 | tf_op jit(solution)/shard_map/ppermute | solution.py:26
  95.3 2.4 %collective-permute-start.5 = (f32[2,3,4,32,4]{4,3,1,0,2:T(8,128)S(1)}, f32[2,3,4,32,4]{4,3,1,0,2:T(8,128)S(1)}, u32[]{:S(2)}, u32[]{:S(2)}) collective-permute-start(f32[2,3,4,32,4]{4,3,1,0,2:T(8,128)S(1)} %get-tuple-element.47), channel_id=1, source_target_pairs={{1,0},{3,2},{5,4},{7,6},{9,8},{11,10},{13,12},{15,14},{17,16},{19,... | collective-permute-start | bytes 36872 | tf_op jit(solution)/shard_map/ppermute | solution.py:29
  97.8 1.5 %collective-permute-start.4 = (f32[2,3,4,32,4]{4,3,1,0,2:T(8,128)S(1)}, f32[2,3,4,32,4]{4,3,1,0,2:T(8,128)S(1)}, u32[]{:S(2)}, u32[]{:S(2)}) collective-permute-start(f32[2,3,4,32,4]{4,3,1,0,2:T(8,128)S(1)} %get-tuple-element.46), channel_id=1, source_target_pairs={{0,1},{2,3},{4,5},{6,7},{8,9},{10,11},{12,13},{14,15},{16,17},{18,... | collective-permute-start | bytes 36872 | tf_op jit(solution)/shard_map/ppermute | solution.py:26
  99.2 7.4 %collective-permute-done.5 = f32[2,3,4,32,4]{4,3,1,0,2:T(8,128)S(1)} collective-permute-done((f32[2,3,4,32,4]{4,3,1,0,2:T(8,128)S(1)}, f32[2,3,4,32,4]{4,3,1,0,2:T(8,128)S(1)}, u32[]{:S(2)}, u32[]{:S(2)}) %collective-permute-start.5) | collective-permute-done | bytes 12320 | tf_op jit(solution)/shard_map/ppermute | solution.py:29
  106.6 4.1 %collective-permute-done.4 = f32[2,3,4,32,4]{4,3,1,0,2:T(8,128)S(1)} collective-permute-done((f32[2,3,4,32,4]{4,3,1,0,2:T(8,128)S(1)}, f32[2,3,4,32,4]{4,3,1,0,2:T(8,128)S(1)}, u32[]{:S(2)}, u32[]{:S(2)}) %collective-permute-start.4) | collective-permute-done | bytes 12320 | tf_op jit(solution)/shard_map/ppermute | solution.py:26
  117.0 0.9 fusion.182
  119.3 1.1 fusion.180
  120.5 0.9 fusion.38
  122.2 0.9 fusion
  123.1 1.0 fusion.64
  124.1 0.9 fusion.1
  (74 shorter events, 18.1 us)
Async XLA Ops:
  0.6 18.0 %collective-permute-start = (f32[2,2,48,768]{3,2,1,0:T(8,128)}, f32[2,2,48,768]{3,2,1,0:T(8,128)S(1)}, u32[]{:S(2)}, u32[]{:S(2)}) collective-permute-start(f32[2,2,48,768]{3,2,1,0:T(8,128)} %param.2), channel_id=1, source_target_pairs={{0,28},{4,0},{8,4},{12,8},{16,12},{20,16},{24,20},{28,24},{1,29},{... | collective-permute-start | bytes 1769480 | tf_op jit(solution)/shard_map/ppermute | solution.py:18
  7.1 11.6 %copy-start = (f32[2,2,48,768]{3,2,1,0:T(8,128)S(1)}, f32[2,2,48,768]{3,2,1,0:T(8,128)}, u32[]{:S(2)}) copy-start(f32[2,2,48,768]{3,2,1,0:T(8,128)} %param.2) | copy-start | bytes 1769476
  18.7 16.9 %collective-permute-start.1 = (f32[2,2,48,768]{3,2,1,0:T(8,128)S(1)}, f32[2,2,48,768]{3,2,1,0:T(8,128)S(1)}, u32[]{:S(2)}, u32[]{:S(2)}) collective-permute-start(f32[2,2,48,768]{3,2,1,0:T(8,128)S(1)} %collective-permute-done), channel_id=1, source_target_pairs={{0,28},{4,0},{8,4},{12,8},{16,12},{20,16},{24,20},{28,24},{1,29},{... | collective-permute-start | bytes 1769480 | tf_op jit(solution)/shard_map/ppermute | solution.py:18
  76.1 13.7 %copy-start.2 = (f32[2,24,96]{2,1,0:T(8,128)S(1)}, f32[2,24,96]{2,1,0:T(8,128)}, u32[]{:S(2)}) copy-start(f32[2,24,96]{2,1,0:T(8,128)} %slice.372) | copy-start | bytes 55300
  76.1 13.7 %copy-start.1 = (f32[2,3,1,24,96]{4,3,1,0,2:T(8,128)S(1)}, f32[2,3,1,24,96]{4,3,1,0,2:T(8,128)}, u32[]{:S(2)}) copy-start(f32[2,3,1,24,96]{4,3,1,0,2:T(8,128)} %broadcast_select_fusion) | copy-start | bytes 165892
  89.9 4.3 %collective-permute-start.3 = (f32[2,3,4,4,96]{4,3,1,0,2:T(4,128)S(1)}, f32[2,3,4,4,96]{4,3,1,0,2:T(4,128)S(1)}, u32[]{:S(2)}, u32[]{:S(2)}) collective-permute-start(f32[2,3,4,4,96]{4,3,1,0,2:T(4,128)S(1)} %get-tuple-element.49), channel_id=1, source_target_pairs={{2,0},{3,1},{6,4},{7,5},{10,8},{11,9},{14,12},{15,13},{18,16},{19,... | collective-permute-start | bytes 110600 | tf_op jit(solution)/shard_map/ppermute | solution.py:29
  91.2 3.9 %collective-permute-start.2 = (f32[2,3,4,4,96]{4,3,1,0,2:T(4,128)S(1)}, f32[2,3,4,4,96]{4,3,1,0,2:T(4,128)S(1)}, u32[]{:S(2)}, u32[]{:S(2)}) collective-permute-start(f32[2,3,4,4,96]{4,3,1,0,2:T(4,128)S(1)} %get-tuple-element.48), channel_id=1, source_target_pairs={{0,2},{1,3},{4,6},{5,7},{8,10},{9,11},{12,14},{13,15},{16,18},{17,... | collective-permute-start | bytes 110600 | tf_op jit(solution)/shard_map/ppermute | solution.py:26
  95.3 11.3 %collective-permute-start.5 = (f32[2,3,4,32,4]{4,3,1,0,2:T(8,128)S(1)}, f32[2,3,4,32,4]{4,3,1,0,2:T(8,128)S(1)}, u32[]{:S(2)}, u32[]{:S(2)}) collective-permute-start(f32[2,3,4,32,4]{4,3,1,0,2:T(8,128)S(1)} %get-tuple-element.47), channel_id=1, source_target_pairs={{1,0},{3,2},{5,4},{7,6},{9,8},{11,10},{13,12},{15,14},{17,16},{19,... | collective-permute-start | bytes 36872 | tf_op jit(solution)/shard_map/ppermute | solution.py:29
  97.8 13.0 %collective-permute-start.4 = (f32[2,3,4,32,4]{4,3,1,0,2:T(8,128)S(1)}, f32[2,3,4,32,4]{4,3,1,0,2:T(8,128)S(1)}, u32[]{:S(2)}, u32[]{:S(2)}) collective-permute-start(f32[2,3,4,32,4]{4,3,1,0,2:T(8,128)S(1)} %get-tuple-element.46), channel_id=1, source_target_pairs={{0,1},{2,3},{4,5},{6,7},{8,9},{10,11},{12,13},{14,15},{16,17},{18,... | collective-permute-start | bytes 36872 | tf_op jit(solution)/shard_map/ppermute | solution.py:26
where the time goes:
time: 131 us; the launch traced here: 130 us
  local copies, waits for them, and re-layouts  43.7 us (33%)
  waiting for transfers between devices  36.7 us (28%)
  other arithmetic  27.8 us (21%)
  matrix products  12.4 us (9%)
  starting transfers between devices  8.82 us (7%)
    ppermute x2, waiting for transfers between devices, shifted(): return lax.ppermute(value, axis, pairs)  24.3 us
    reduce_sum x2, other arithmetic, multilook(): return blocks.mean(axis=(-3, -1))  21.1 us
    add x1, local copies, waits for them, and re-layouts, body(): window[:, 0] * window[:, 0] + window[:, 1] * window[:, 1]  9.54 us
    squeeze x1, local copies, waits for them, and re-layouts, body(): partners[:, :, 1]  9.54 us
    squeeze x1, local copies, waits for them, and re-layouts, body(): partners[:, :, 0]  9.4 us
    ppermute x2, waiting for transfers between devices, with_halo(): lax.ppermute(lax.slice_in_dim(block, 0, width, axis=dim), axis, backward)  7.37 us
    dot_general x8, matrix products, along_cols(): return jnp.einsum('vx,...ybx->...ybv', table, values, precision=highest)  6.68 us
    dot_general x8, matrix products, along_rows(): return jnp.einsum('uy,...ybx->...ubx', table, values, precision=highest)  5.71 us
  transfers between devices with their start and end apart: 6, of which 5 were waited for; matrix products, arithmetic and copies ran while one was open for 8% of the time, Pallas kernels for 0%

commit v1 on v0

v1 whole, which is shorter than its diff:
```python
import functools
import math

import jax
import jax.numpy as jnp
import ml_dtypes
import numpy as np
from jax import lax
from jax.experimental import pallas as pl
from jax.experimental.pallas import tpu as pltpu
from jax.sharding import PartitionSpec as P

LOOK_R = 2
LOOK_C = 8
PATCH = 32
KEEP = 24
MARGIN = 4
LANES = 128
BAND = 8
MESH = pl.DeviceIdType.MESH
HIGHEST = lax.Precision.HIGHEST


def tables(rows, cols):
    cells_r, cells_c = rows // LOOK_R, cols // LOOK_C
    blocks = cells_c // KEEP
    halo_r = MARGIN * LOOK_R
    tall = rows + 2 * halo_r

    looks = np.zeros((cols, LANES), np.float32)
    looks[np.arange(cols), np.arange(cols) // LOOK_C] = 1.0 / (LOOK_R * LOOK_C)

    def lane(x):
        if x < 0:
            return cells_c + MARGIN + x
        return x if x < cells_c else x + MARGIN

    ticks = np.arange(PATCH)
    angle = (ticks[:, None] * ticks[None, :] % PATCH) * (2.0 * math.pi / PATCH)
    cosine, sine = np.cos(angle), np.sin(angle)

    pick = np.zeros((PATCH, tall))
    pick[np.arange(tall) // LOOK_R, np.arange(tall)] = 1.0
    row_c, row_s = cosine @ pick, sine @ pick
    box_r = np.zeros((cells_r, PATCH))
    for y in range(cells_r):
        box_r[y, MARGIN + y - 1 : MARGIN + y + 2] = 1.0
    box_r = box_r @ pick
    none = np.zeros_like(box_r)
    row_fwd = np.block([[row_c, row_s], [-row_s, row_c], [box_r, none], [none, box_r]])

    col_c, col_s = np.zeros((LANES, LANES)), np.zeros((LANES, LANES))
    for b in range(blocks):
        for x in range(PATCH):
            at = lane(b * KEEP - MARGIN + x)
            col_c[at, b * PATCH : (b + 1) * PATCH] = cosine[x]
            col_s[at, b * PATCH : (b + 1) * PATCH] = sine[x]
    col_fwd = np.block([[col_c, -col_s], [col_s, col_c]])
    box_c = np.zeros((LANES, LANES))
    for x in range(cells_c):
        for step in (-1, 0, 1):
            box_c[lane(x + step), x] = 1.0

    group = np.kron(np.eye(LANES // PATCH), np.ones((PATCH, PATCH)))

    centre = slice(MARGIN, MARGIN + KEEP)
    row_inv = np.block([[cosine[centre], -sine[centre]], [sine[centre], cosine[centre]]])
    inv_c, inv_s = np.zeros((LANES, LANES)), np.zeros((LANES, LANES))
    for b in range(blocks):
        inv_c[b * PATCH : (b + 1) * PATCH, b * KEEP : (b + 1) * KEEP] = cosine[:, centre]
        inv_s[b * PATCH : (b + 1) * PATCH, b * KEEP : (b + 1) * KEEP] = sine[:, centre]
    col_inv = np.block([[inv_c, inv_s], [-inv_s, inv_c]]) / (PATCH * PATCH)
    single = [row_fwd, box_r, col_fwd, box_c, group, row_inv, col_inv]
    return [looks.astype(ml_dtypes.bfloat16)] + [np.asarray(t, np.float32) for t in single]


def dot(a, b):
    return lax.dot_general(
        a, b, (((1,), (0,)), ((), ())), precision=HIGHEST, preferred_element_type=jnp.float32
    )


def kernel(
    sizes,
    offs_ref,
    img_ref,
    looks_ref,
    row_fwd_ref,
    box_r_ref,
    col_fwd_ref,
    box_c_ref,
    group_ref,
    row_inv_ref,
    col_inv_ref,
    filt_ref,
    coh_ref,
    near,
    far,
    planes,
    edge_l,
    edge_r,
    side_l,
    side_r,
    near_send,
    near_recv,
    far_send,
    far_recv,
    halo_send,
    halo_recv,
):
    dates, n_rows, n_cols = sizes
    rows, cols = img_ref.shape[2], img_ref.shape[3]
    cells_c = cols // LOOK_C
    cells_r = rows // LOOK_R
    halo = MARGIN * LOOK_R
    chunks = rows // BAND
    date, row, col = lax.axis_index("date"), lax.axis_index("row"), lax.axis_index("col")
    odd = lax.rem(date, 2) == 1
    mate = date + 1 - 2 * lax.rem(date, 2)
    before = lax.rem(date + dates - 2, dates)
    after = lax.rem(date + 2, dates)
    steps = [(r, c) for r in (-1, 0, 1) for c in (-1, 0, 1) if (r, c) != (0, 0)]

    def there(step):
        test_r = [None, row < n_rows - 1, row > 0][step[0]]
        test_c = [None, col < n_cols - 1, col > 0][step[1]]
        tests = [t for t in (test_r, test_c) if t is not None]
        return functools.reduce(jnp.logical_and, tests)

    barrier = pltpu.get_barrier_semaphore()
    for other in (before, after, mate):
        pl.semaphore_signal(barrier, inc=1, device_id=(other, row, col), device_id_type=MESH)
    count = jnp.int32(3)
    for step in steps:
        here = there(step)

        @pl.when(here)
        def _():
            pl.semaphore_signal(
                barrier,
                inc=1,
                device_id=(date, row + step[0], col + step[1]),
                device_id_type=MESH,
            )

        count = count + here.astype(jnp.int32)
    pl.semaphore_wait(barrier, count)

    def band(c):
        return pl.ds(c * BAND, BAND)

    def far_copy(c):
        return pltpu.make_async_remote_copy(
            src_ref=img_ref.at[:, :, band(c)],
            dst_ref=far.at[:, :, band(c)],
            send_sem=far_send.at[c],
            recv_sem=far_recv.at[c],
            device_id=(before, row, col),
            device_id_type=MESH,
        )

    def near_copy(c, source):
        return pltpu.make_async_remote_copy(
            src_ref=source.at[:, :, band(c)],
            dst_ref=near.at[:, :, band(c)],
            send_sem=near_send.at[c],
            recv_sem=near_recv.at[c],
            device_id=(mate, row, col),
            device_id_type=MESH,
        )

    for c in range(chunks):
        far_copy(c).start()

        @pl.when(odd)
        def _():
            near_copy(c, img_ref).start()

    for step in steps:

        @pl.when(jnp.logical_not(there(step)))
        def _():
            r, c = step
            at = {-1: slice(0, halo), 0: slice(halo, halo + rows), 1: slice(halo + rows, None)}[r]
            if c == 0:
                planes[:, at] = jnp.zeros_like(planes[:, at])
            else:
                side = side_l if c < 0 else side_r
                side[at] = jnp.zeros_like(side[at])

    first = [[offs_ref[k, l] == l + 1 for l in range(3)] for k in range(2)]

    def process(c):
        at = band(c)

        def date_image(i):
            source = (img_ref, near, far)[i // 2]
            return source[i % 2, 0, at], source[i % 2, 1, at]

        images = [date_image(i) for i in range(6)]
        parts = []
        for k in range(2):
            a_r, a_i = images[k]
            for l in range(3):
                low, high = images[k + l + 1], images[k + l + 2]
                b_r = jnp.where(first[k][l], low[0], high[0])
                b_i = jnp.where(first[k][l], low[1], high[1])
                parts += [a_r * b_r + a_i * b_i, a_i * b_r - a_r * b_i]
        parts += [r * r + i * i for r, i in images]
        stacked = jnp.concatenate(parts, axis=0)
        high = stacked.astype(jnp.bfloat16)
        low = (stacked - high.astype(jnp.float32)).astype(jnp.bfloat16)
        looks = looks_ref[...]
        summed = jnp.dot(high, looks, preferred_element_type=jnp.float32) + jnp.dot(
            low, looks, preferred_element_type=jnp.float32
        )
        for p in range(len(parts)):
            planes[p, pl.ds(halo + c * BAND, BAND)] = summed[p * BAND : (p + 1) * BAND]

    for c in range(chunks):
        far_copy(c).wait_recv()

        @pl.when(jnp.logical_not(odd))
        def _():
            near_copy(c, far).start()

        near_copy(c, img_ref).wait_recv()
        process(c)

    count_planes = planes.shape[0]
    lanes = lax.broadcasted_iota(jnp.int32, (rows, LANES), 1)
    pack_l = jnp.zeros((rows, LANES), jnp.float32)
    pack_r = jnp.zeros((rows, LANES), jnp.float32)
    for p in range(count_planes):
        own = planes[p, halo : halo + rows]
        mine = (lanes >= p * MARGIN) & (lanes < (p + 1) * MARGIN)
        pack_l = jnp.where(mine, pltpu.roll(own, (p * MARGIN) % LANES, 1), pack_l)
        shift = (p * MARGIN - (cells_c - MARGIN)) % LANES
        pack_r = jnp.where(mine, pltpu.roll(own, shift, 1), pack_r)
    edge_l[...] = pack_l
    edge_r[...] = pack_r

    def halo_copy(n, step):
        r, c = step
        source_rows = {-1: slice(0, halo), 0: slice(0, rows), 1: slice(rows - halo, rows)}[r]
        target_rows = {
            -1: slice(halo + rows, rows + 2 * halo),
            0: slice(halo, halo + rows),
            1: slice(0, halo),
        }[r]
        if c == 0:
            shifted = slice(source_rows.start + halo, source_rows.stop + halo)
            source, target = planes.at[:, shifted], planes.at[:, target_rows]
        elif c < 0:
            source, target = edge_l.at[source_rows], side_r.at[target_rows]
        else:
            source, target = edge_r.at[source_rows], side_l.at[target_rows]
        return pltpu.make_async_remote_copy(
            src_ref=source,
            dst_ref=target,
            send_sem=halo_send.at[n],
            recv_sem=halo_recv.at[n],
            device_id=(date, row + r, col + c),
            device_id_type=MESH,
        )

    for n, step in enumerate(steps):

        @pl.when(there(step))
        def _():
            halo_copy(n, step).start()

    for n, step in enumerate(steps):
        @pl.when(there((-step[0], -step[1])))
        def _():
            halo_copy(n, step).wait_recv()

    tall = rows + 2 * halo
    wide = lax.broadcasted_iota(jnp.int32, (tall, LANES), 1)
    in_l = (wide >= cells_c) & (wide < cells_c + MARGIN)
    in_r = (wide >= cells_c + MARGIN) & (wide < cells_c + 2 * MARGIN)
    got_l, got_r = side_l[...], side_r[...]

    def whole(p):
        left = pltpu.roll(got_l, (cells_c - p * MARGIN) % LANES, 1)
        right = pltpu.roll(got_r, (cells_c + MARGIN - p * MARGIN) % LANES, 1)
        return jnp.where(in_l, left, jnp.where(in_r, right, planes[p]))

    row_fwd, box_r = row_fwd_ref[...], box_r_ref[...]
    spectra, boxes = [], []
    for p in range(6):
        both = jnp.concatenate([whole(2 * p), whole(2 * p + 1)], axis=0)
        out = dot(row_fwd, both)
        spectra.append(jnp.concatenate([out[:PATCH], out[PATCH : 2 * PATCH]], axis=1))
        boxes.append(out[2 * PATCH :])
    for p in range(12, 18):
        boxes.append(dot(box_r, whole(p)))
    box = dot(jnp.concatenate(boxes, axis=0), box_c_ref[...]) * (1.0 / 9.0)
    base = 12 * cells_r
    power = [box[base + i * cells_r : base + (i + 1) * cells_r] for i in range(6)]
    for k in range(2):
        for l in range(3):
            second = jnp.where(first[k][l], power[k + l + 1], power[k + l + 2])
            factor = lax.rsqrt(power[k] * second + 1e-06)
            for part in range(2):
                at = ((k * 3 + l) * 2 + part) * cells_r
                coh_ref[k, l, part] = (box[at : at + cells_r] * factor)[:, :cells_c]

    z = dot(jnp.concatenate(spectra, axis=0), col_fwd_ref[...])
    z_r, z_i = z[:, :LANES], z[:, LANES:]
    energy = z_r * z_r + z_i * z_i
    group = group_ref[...]
    lane32 = lax.rem(lax.broadcasted_iota(jnp.int32, (6 * PATCH, LANES), 1), PATCH)
    left = jnp.where(lane32 == 0, pltpu.roll(energy, LANES - PATCH + 1, 1), pltpu.roll(energy, 1, 1))
    right = jnp.where(
        lane32 == PATCH - 1, pltpu.roll(energy, PATCH - 1, 1), pltpu.roll(energy, LANES - 1, 1)
    )
    across = energy + left + right

    def per_patch(values):
        sums = [
            jnp.sum(values[p * PATCH : (p + 1) * PATCH], axis=0, keepdims=True) for p in range(6)
        ]
        sums += [jnp.zeros((2, LANES), jnp.float32)]
        return dot(jnp.concatenate(sums, axis=0), group) * (1.0 / (PATCH * PATCH))

    level = per_patch(energy)
    weights = []
    for p in range(6):
        part = across[p * PATCH : (p + 1) * PATCH]
        smooth = (part + pltpu.roll(part, 1, 0) + pltpu.roll(part, PATCH - 1, 0)) * (1.0 / 9.0)
        weights.append(jnp.sqrt(jnp.sqrt(smooth + level[p : p + 1] + 1e-06)))
    scale = 1.0 / per_patch(jnp.concatenate(weights, axis=0))
    row_inv = row_inv_ref[...]
    back = []
    for p in range(6):
        weight = weights[p] * scale[p : p + 1]
        at = slice(p * PATCH, (p + 1) * PATCH)
        both = jnp.concatenate([z_r[at] * weight, z_i[at] * weight], axis=0)
        out = dot(row_inv, both)
        back.append(jnp.concatenate([out[:KEEP], out[KEEP:]], axis=1))
    final = dot(jnp.concatenate(back, axis=0), col_inv_ref[...])
    for p in range(6):
        at = slice(p * KEEP, (p + 1) * KEEP)
        filt_ref[p // 3, p % 3, 0] = final[at, :cells_c]
        filt_ref[p // 3, p % 3, 1] = final[at, LANES : LANES + cells_c]

    for c in range(chunks):
        far_copy(c).wait_send()
        near_copy(c, img_ref).wait_send()
    for n, step in enumerate(steps):

        @pl.when(there(step))
        def _():
            halo_copy(n, step).wait_send()


def body(images, secondaries):
    per_device, _, rows, cols = images.shape
    links = secondaries.shape[1]
    dates = lax.axis_size("date")
    assert per_device == 2 and links == 3 and rows == 2 * KEEP and dates % 2 == 0 and dates > 4
    own = lax.axis_index("date") * per_device + jnp.arange(per_device, dtype=jnp.int32)
    offsets = (secondaries - own[:, None]) % (per_device * dates)
    cells_r, cells_c = rows // LOOK_R, cols // LOOK_C
    tall = rows + 2 * MARGIN * LOOK_R
    chunks = rows // BAND
    out = jax.ShapeDtypeStruct((per_device, links, 2, cells_r, cells_c), jnp.float32)
    constants = [jnp.asarray(t) for t in tables(rows, cols)]
    vmem = pl.BlockSpec(memory_space=pltpu.VMEM)
    sizes = (dates, lax.axis_size("row"), lax.axis_size("col"))
    dma = pltpu.SemaphoreType.DMA
    return pl.pallas_call(
        functools.partial(kernel, sizes),
        out_shape=(out, out),
        in_specs=[pl.BlockSpec(memory_space=pltpu.SMEM)] + [vmem] * (1 + len(constants)),
        out_specs=(vmem, vmem),
        scratch_shapes=[
            pltpu.VMEM(images.shape, jnp.float32),
            pltpu.VMEM(images.shape, jnp.float32),
            pltpu.VMEM((18, tall, LANES), jnp.float32),
            pltpu.VMEM((rows, LANES), jnp.float32),
            pltpu.VMEM((rows, LANES), jnp.float32),
            pltpu.VMEM((tall, LANES), jnp.float32),
            pltpu.VMEM((tall, LANES), jnp.float32),
            dma((chunks,)),
            dma((chunks,)),
            dma((chunks,)),
            dma((chunks,)),
            dma((8,)),
            dma((8,)),
        ],
        compiler_params=pltpu.CompilerParams(
            collective_id=0, has_side_effects=True, vmem_limit_bytes=32 * 1024 * 1024
        ),
        cost_estimate=pl.CostEstimate(flops=10**9, bytes_accessed=10**6, transcendentals=0),
    )(offsets, images, *constants)


def solution(mesh):
    in_specs = (P("date", None, "row", "col"), P("date", None))
    out_specs = (P("date", None, None, "row", "col"), P("date", None, None, "row", "col"))
    return jax.shard_map(body, mesh=mesh, in_specs=in_specs, out_specs=out_specs, check_vma=False)
```

time: 131 us -> 38.2 us (0.29)
  the two profiles are of different devices: /device:TPU:30 before, /device:TPU:3 now
where the time goes in v1:
time: 38.2 us; the launch traced here: 37.7 us
  Pallas kernels  27.8 us (73%)
  local copies, waits for them, and re-layouts  8.42 us (22%)
  other arithmetic  0.76 us (2%)
  between operations  0.67 us (2%)
    pallas_call x1, Pallas kernels, body(): pl.pallas_call(functools.partial(kernel, sizes), out_shape=(out, out), in...  27.8 us
    unnamed x20, local copies, waits for them, and re-layouts  8.42 us

profile of v1, /device:TPU:3, one launch (start us, length us, event | category | flops | bytes accessed | tf_op | source)
XLA Modules:
  0.0 37.7 jit_solution(11082732836759785677)
XLA Ops:
  0.6 0.0 copy-start.7
  0.7 0.8 %and_select_fusion.offs_ref = s32[2,3]{1,0:T(2,128)S(1)} fusion(s32[2,3]{1,0:T(2,128)} %param.11, s32[2]{0:T(128)S(1)} %iota_add_fusion), kind=kLoop, calls=%fused_computation.2 | loop fusion | flops 72 | bytes 56 | tf_op jit(solution)/shard_map/jit(remainder)/select_n | solution.py:364
  1.4 0.0 copy-done.7
  1.4 0.0 copy-start
  1.4 1.1 %copy-done = f32[2,2,48,768]{3,2,1,0:T(8,128)S(1)} copy-done((f32[2,2,48,768]{3,2,1,0:T(8,128)S(1)}, f32[2,2,48,768]{3,2,1,0:T(8,128)}, u32[]{:S(2)}) %copy-start) | copy-done | bytes 589848
  2.5 0.0 copy-start.1
  2.5 0.9 %copy-done.1 = f32[256,256]{1,0:T(8,128)S(1)} copy-done((f32[256,256]{1,0:T(8,128)S(1)}, f32[256,256]{1,0:T(8,128)}, u32[]{:S(2)}) %copy-start.1) | copy-done | bytes 262168
  3.4 0.0 copy-start.2
  3.4 0.9 %copy-done.2 = f32[256,256]{1,0:T(8,128)S(1)} copy-done((f32[256,256]{1,0:T(8,128)S(1)}, f32[256,256]{1,0:T(8,128)}, u32[]{:S(2)}) %copy-start.2) | copy-done | bytes 262168
  4.4 0.0 copy-start.3
  4.4 0.9 %copy-done.3 = bf16[768,128]{1,0:T(8,128)(2,1)S(1)} copy-done((bf16[768,128]{1,0:T(8,128)(2,1)S(1)}, bf16[768,128]{1,0:T(8,128)(2,1)}, u32[]{:S(2)}) %copy-start.3) | copy-done | bytes 196632
  5.3 0.0 copy-start.4
  5.3 0.8 %copy-done.4 = f32[128,128]{1,0:T(8,128)S(1)} copy-done((f32[128,128]{1,0:T(8,128)S(1)}, f32[128,128]{1,0:T(8,128)}, u32[]{:S(2)}) %copy-start.4) | copy-done | bytes 65560
  6.2 0.0 copy-start.5
  6.2 0.8 %copy-done.5 = f32[128,128]{1,0:T(8,128)S(1)} copy-done((f32[128,128]{1,0:T(8,128)S(1)}, f32[128,128]{1,0:T(8,128)}, u32[]{:S(2)}) %copy-start.5) | copy-done | bytes 65560
  7.0 0.0 copy-start.6
  7.0 0.8 %copy-done.6 = f32[112,128]{1,0:T(8,128)S(1)} copy-done((f32[112,128]{1,0:T(8,128)S(1)}, f32[112,128]{1,0:T(8,128)}, u32[]{:S(2)}) %copy-start.6) | copy-done | bytes 57368
  7.8 0.0 copy-start.8
  7.8 0.7 %copy-done.8 = f32[24,64]{1,0:T(8,128)S(1)} copy-done((f32[24,64]{1,0:T(8,128)S(1)}, f32[24,64]{1,0:T(8,128)}, u32[]{:S(2)}) %copy-start.8) | copy-done | bytes 6168
  8.5 27.8 %shard_map.113 = (f32[2,3,2,24,96]{4,3,2,1,0:T(8,128)S(1)}, f32[2,3,2,24,96]{4,3,2,1,0:T(8,128)S(1)}) custom-call(s32[2,3]{1,0:T(2,128)S(1)} %and_select_fusion.offs_ref, f32[2,2,48,768]{3,2,1,0:T(8,128)S(1)} %copy-done, bf16[768,128]{1,0:T(8,128)(2,1)S(1)} %copy-done.3, f32[112,128]{1,0:T(8,128)S(1)} %copy-done.6, f32[24,64]{1,0:T(8,128)S(1)} %copy-done.8, ...), custom_call_target="tpu_custom_call" | custom-call | flops 1000000000 | bytes 1000000 | tf_op jit(solution)/shard_map/pallas_call | solution.py:373
  36.3 0.7 %copy.14 = f32[2,3,2,24,96]{4,3,2,1,0:T(8,128)} copy(f32[2,3,2,24,96]{4,3,2,1,0:T(8,128)S(1)} %get-tuple-element.4) | data formatting | bytes 221184
  37.0 0.7 %copy.15 = f32[2,3,2,24,96]{4,3,2,1,0:T(8,128)} copy(f32[2,3,2,24,96]{4,3,2,1,0:T(8,128)S(1)} %get-tuple-element.5) | data formatting | bytes 221184
  (1 shorter events, 0.0 us)
Async XLA Ops:
  0.6 0.8 %copy-start.7 = (f32[48,64]{1,0:T(8,128)S(1)}, f32[48,64]{1,0:T(8,128)}, u32[]{:S(2)}) copy-start(f32[48,64]{1,0:T(8,128)} %constant.45.clone.row_inv_ref) | copy-start | bytes 36868
  1.4 1.1 %copy-start = (f32[2,2,48,768]{3,2,1,0:T(8,128)S(1)}, f32[2,2,48,768]{3,2,1,0:T(8,128)}, u32[]{:S(2)}) copy-start(f32[2,2,48,768]{3,2,1,0:T(8,128)} %img_ref.1) | copy-start | bytes 1769476
  2.5 0.9 %copy-start.1 = (f32[256,256]{1,0:T(8,128)S(1)}, f32[256,256]{1,0:T(8,128)}, u32[]{:S(2)}) copy-start(f32[256,256]{1,0:T(8,128)} %constant.46.clone.col_inv_ref) | copy-start | bytes 786436
  3.4 0.9 %copy-start.2 = (f32[256,256]{1,0:T(8,128)S(1)}, f32[256,256]{1,0:T(8,128)}, u32[]{:S(2)}) copy-start(f32[256,256]{1,0:T(8,128)} %constant.42.clone.col_fwd_ref) | copy-start | bytes 786436
  4.4 0.9 %copy-start.3 = (bf16[768,128]{1,0:T(8,128)(2,1)S(1)}, bf16[768,128]{1,0:T(8,128)(2,1)}, u32[]{:S(2)}) copy-start(bf16[768,128]{1,0:T(8,128)(2,1)} %constant.39.clone.looks_ref) | copy-start | bytes 589828
  5.3 0.8 %copy-start.4 = (f32[128,128]{1,0:T(8,128)S(1)}, f32[128,128]{1,0:T(8,128)}, u32[]{:S(2)}) copy-start(f32[128,128]{1,0:T(8,128)} %constant.44.clone.group_ref) | copy-start | bytes 196612
  6.2 0.8 %copy-start.5 = (f32[128,128]{1,0:T(8,128)S(1)}, f32[128,128]{1,0:T(8,128)}, u32[]{:S(2)}) copy-start(f32[128,128]{1,0:T(8,128)} %constant.43.clone.box_c_ref) | copy-start | bytes 196612
  7.0 0.8 %copy-start.6 = (f32[112,128]{1,0:T(8,128)S(1)}, f32[112,128]{1,0:T(8,128)}, u32[]{:S(2)}) copy-start(f32[112,128]{1,0:T(8,128)} %constant.40.clone.row_fwd_ref) | copy-start | bytes 172036
  7.8 0.7 %copy-start.8 = (f32[24,64]{1,0:T(8,128)S(1)}, f32[24,64]{1,0:T(8,128)}, u32[]{:S(2)}) copy-start(f32[24,64]{1,0:T(8,128)} %constant.41.clone.box_r_ref) | copy-start | bytes 18436

commit v2 on v1

v2 whole, which is shorter than its diff:
```python
import functools
import math

import jax
import jax.numpy as jnp
import ml_dtypes
import numpy as np
from jax import lax
from jax.experimental import pallas as pl
from jax.experimental.pallas import tpu as pltpu
from jax.sharding import PartitionSpec as P

LOOK_R = 2
LOOK_C = 8
PATCH = 32
KEEP = 24
MARGIN = 4
LANES = 128
BAND = 8
MESH = pl.DeviceIdType.MESH


def tables(rows, cols):
    cells_r, cells_c = rows // LOOK_R, cols // LOOK_C
    blocks = cells_c // KEEP
    halo_r = MARGIN * LOOK_R
    tall = rows + 2 * halo_r

    def lane(x):
        if x < 0:
            return cells_c + MARGIN + x
        return x if x < cells_c else x + MARGIN

    ticks = np.arange(PATCH)
    angle = (ticks[:, None] * ticks[None, :] % PATCH) * (2.0 * math.pi / PATCH)
    cosine, sine = np.cos(angle), np.sin(angle)

    pick = np.zeros((PATCH, tall))
    pick[np.arange(tall) // LOOK_R, np.arange(tall)] = 1.0
    row_c, row_s = cosine @ pick, sine @ pick
    box_r = np.zeros((cells_r, PATCH))
    for y in range(cells_r):
        box_r[y, MARGIN + y - 1 : MARGIN + y + 2] = 1.0
    box_r = box_r @ pick
    none = np.zeros_like(box_r)
    row_fwd = np.block([[row_c, row_s], [-row_s, row_c], [box_r, none], [none, box_r]])

    col_c, col_s = np.zeros((LANES, LANES)), np.zeros((LANES, LANES))
    for b in range(blocks):
        for x in range(PATCH):
            at = lane(b * KEEP - MARGIN + x)
            col_c[at, b * PATCH : (b + 1) * PATCH] = cosine[x]
            col_s[at, b * PATCH : (b + 1) * PATCH] = sine[x]
    centre = slice(MARGIN, MARGIN + KEEP)
    row_inv = np.block([[cosine[centre], -sine[centre]], [sine[centre], cosine[centre]]])
    inv_c, inv_s = np.zeros((LANES, LANES)), np.zeros((LANES, LANES))
    for b in range(blocks):
        inv_c[b * PATCH : (b + 1) * PATCH, b * KEEP : (b + 1) * KEEP] = cosine[:, centre]
        inv_s[b * PATCH : (b + 1) * PATCH, b * KEEP : (b + 1) * KEEP] = sine[:, centre]
    scale = 1.0 / (PATCH * PATCH)
    row_inv = np.pad(row_inv, ((0, 0), (0, LANES - 2 * PATCH)))
    stacked = [row_fwd, col_c, col_s, inv_c * scale, inv_s * scale, row_inv]
    whole = np.concatenate(stacked, axis=0).astype(np.float32)
    high = whole.astype(ml_dtypes.bfloat16)
    low = (whole - high.astype(np.float32)).astype(ml_dtypes.bfloat16)
    starts = np.cumsum([0] + [t.shape[0] for t in stacked])
    return np.stack([high, low]), [int(n) for n in starts]


def split(x):
    high = x.astype(jnp.bfloat16)
    return high, (x - high.astype(jnp.float32)).astype(jnp.bfloat16)


def mul(a, b):
    return lax.dot_general(a, b, (((1,), (0,)), ((), ())), preferred_element_type=jnp.float32)


def dot(a, b):
    return mul(a[0], b[0]) + (mul(a[1], b[0]) + mul(a[0], b[1]))


def dot_exact(x, b):
    high, low = split(x)
    return mul(high, b) + mul(low, b)


def kernel(
    sizes,
    starts,
    sec_ref,
    img_hbm,
    table_hbm,
    filt_ref,
    coh_ref,
    img_ref,
    table,
    near,
    far,
    planes,
    edge_l,
    edge_r,
    side_l,
    side_r,
    near_send,
    near_recv,
    far_send,
    far_recv,
    halo_send,
    halo_recv,
    local_sem,
):
    dates, n_rows, n_cols = sizes
    rows, cols = img_ref.shape[2], img_ref.shape[3]
    cells_c = cols // LOOK_C
    cells_r = rows // LOOK_R
    halo = MARGIN * LOOK_R
    chunks = rows // BAND
    date, row, col = lax.axis_index("date"), lax.axis_index("row"), lax.axis_index("col")
    odd = lax.rem(date, 2) == 1
    mate = date + 1 - 2 * lax.rem(date, 2)
    before = lax.rem(date + dates - 2, dates)
    after = lax.rem(date + 2, dates)
    steps = [(r, c) for r in (-1, 0, 1) for c in (-1, 0, 1) if (r, c) != (0, 0)]

    def there(step):
        test_r = [None, row < n_rows - 1, row > 0][step[0]]
        test_c = [None, col < n_cols - 1, col > 0][step[1]]
        tests = [t for t in (test_r, test_c) if t is not None]
        return functools.reduce(jnp.logical_and, tests)

    order = [0, chunks - 1] + list(range(1, chunks - 1))
    load_img = pltpu.make_async_copy(img_hbm, img_ref, local_sem.at[0])
    load_table = pltpu.make_async_copy(table_hbm, table, local_sem.at[1])
    load_img.start()
    load_table.start()
    barrier = pltpu.get_barrier_semaphore()
    for other in (before, after, mate):
        pl.semaphore_signal(barrier, inc=1, device_id=(other, row, col), device_id_type=MESH)
    count = jnp.int32(3)
    for step in steps:
        here = there(step)

        @pl.when(here)
        def _():
            pl.semaphore_signal(
                barrier,
                inc=1,
                device_id=(date, row + step[0], col + step[1]),
                device_id_type=MESH,
            )

        count = count + here.astype(jnp.int32)
    pl.semaphore_wait(barrier, count)

    def band(c):
        return pl.ds(c * BAND, BAND)

    def far_copy(c):
        return pltpu.make_async_remote_copy(
            src_ref=img_hbm.at[:, :, band(c)],
            dst_ref=far.at[:, :, band(c)],
            send_sem=far_send.at[c],
            recv_sem=far_recv.at[c],
            device_id=(before, row, col),
            device_id_type=MESH,
        )

    def near_copy(c, source):
        return pltpu.make_async_remote_copy(
            src_ref=source.at[:, :, band(c)],
            dst_ref=near.at[:, :, band(c)],
            send_sem=near_send.at[c],
            recv_sem=near_recv.at[c],
            device_id=(mate, row, col),
            device_id_type=MESH,
        )

    for c in order:
        far_copy(c).start()

        @pl.when(odd)
        def _():
            near_copy(c, img_hbm).start()

    for step in steps:

        @pl.when(jnp.logical_not(there(step)))
        def _():
            r, c = step
            at = {-1: slice(0, halo), 0: slice(halo, halo + rows), 1: slice(halo + rows, None)}[r]
            if c == 0:
                planes[:, at] = jnp.zeros_like(planes[:, at])
            else:
                side = side_l if c < 0 else side_r
                side[at] = jnp.zeros_like(side[at])

    total = 2 * dates

    def is_first(k, l):
        return lax.rem(sec_ref[k, l] - (2 * date + k) + total, total) == l + 1

    first = [[is_first(k, l) for l in range(3)] for k in range(2)]

    def lane_of(x):
        return jnp.where(x < 0, cells_c + MARGIN + x, jnp.where(x < cells_c, x, x + MARGIN))

    cell = lax.broadcasted_iota(jnp.int32, (cols, LANES), 0) // LOOK_C
    looks = jnp.where(
        cell == lax.broadcasted_iota(jnp.int32, (cols, LANES), 1), 1.0 / (LOOK_R * LOOK_C), 0.0
    ).astype(jnp.bfloat16)
    from_lane = lax.broadcasted_iota(jnp.int32, (LANES, LANES), 0)
    to_lane = lax.broadcasted_iota(jnp.int32, (LANES, LANES), 1)
    box_c = (from_lane == to_lane) | (from_lane == lane_of(to_lane - 1))
    box_c = box_c | (from_lane == lane_of(to_lane + 1))
    box_c = jnp.where(box_c & (to_lane < cells_c), 1.0, 0.0).astype(jnp.bfloat16)
    group = jnp.where(from_lane // PATCH == to_lane // PATCH, 1.0, 0.0).astype(jnp.bfloat16)

    def process(c):
        at = band(c)

        def date_image(i):
            source = (img_ref, near, far)[i // 2]
            return source[i % 2, 0, at], source[i % 2, 1, at]

        images = [date_image(i) for i in range(6)]
        parts = []
        for k in range(2):
            a_r, a_i = images[k]
            for l in range(3):
                low, high = images[k + l + 1], images[k + l + 2]
                b_r = jnp.where(first[k][l], low[0], high[0])
                b_i = jnp.where(first[k][l], low[1], high[1])
                parts += [a_r * b_r + a_i * b_i, a_i * b_r - a_r * b_i]
        parts += [r * r + i * i for r, i in images]
        summed = dot_exact(jnp.concatenate(parts, axis=0), looks)
        lanes = lax.broadcasted_iota(jnp.int32, (BAND, LANES), 1)
        pack_l = jnp.zeros((BAND, LANES), jnp.float32)
        pack_r = jnp.zeros((BAND, LANES), jnp.float32)
        for p in range(len(parts)):
            own = summed[p * BAND : (p + 1) * BAND]
            planes[p, pl.ds(halo + c * BAND, BAND)] = own
            mine = (lanes >= p * MARGIN) & (lanes < (p + 1) * MARGIN)
            pack_l = jnp.where(mine, pltpu.roll(own, (p * MARGIN) % LANES, 1), pack_l)
            shift = (p * MARGIN - (cells_c - MARGIN)) % LANES
            pack_r = jnp.where(mine, pltpu.roll(own, shift, 1), pack_r)
        edge_l[at] = pack_l
        edge_r[at] = pack_r

    messages = []
    for step in steps:
        if step[0] == 0:
            messages += [(step, c * BAND, BAND, c) for c in range(chunks)]
        else:
            c = 0 if step[0] < 0 else chunks - 1
            messages.append((step, c * BAND, BAND, c))

    def halo_copy(n):
        (r, c), start, size, _ = messages[n]
        source_at = pl.ds(start, size)
        target_at = pl.ds(halo + start - r * rows, size)
        if c == 0:
            source, target = planes.at[:, pl.ds(halo + start, size)], planes.at[:, target_at]
        elif c < 0:
            source, target = edge_l.at[source_at], side_r.at[target_at]
        else:
            source, target = edge_r.at[source_at], side_l.at[target_at]
        return pltpu.make_async_remote_copy(
            src_ref=source,
            dst_ref=target,
            send_sem=halo_send.at[n],
            recv_sem=halo_recv.at[n],
            device_id=(date, row + r, col + c),
            device_id_type=MESH,
        )

    load_img.wait()
    for c in order:
        far_copy(c).wait_recv()

        @pl.when(jnp.logical_not(odd))
        def _():
            near_copy(c, far).start()

        near_copy(c, img_hbm).wait_recv()
        process(c)
        for step in steps:

            @pl.when(there(step))
            def _():
                for n, message in enumerate(messages):
                    if message[0] == step and message[3] == c:
                        halo_copy(n).start()

    load_table.wait()

    def part_of(i, j, lanes=LANES):
        rows_at = slice(starts[i], starts[j])
        return table[0, rows_at, :lanes], table[1, rows_at, :lanes]

    row_fwd = part_of(0, 1)
    box_r = table[0, starts[0] + 2 * PATCH : starts[0] + 2 * PATCH + cells_r, : rows + 2 * halo]
    col_fwd = [
        jnp.concatenate(
            [
                jnp.concatenate([cosine, -sine], axis=1),
                jnp.concatenate([sine, cosine], axis=1),
            ],
            axis=0,
        )
        for cosine, sine in zip(part_of(1, 2), part_of(2, 3))
    ]
    col_inv = [
        jnp.concatenate(
            [
                jnp.concatenate([cosine, sine], axis=1),
                jnp.concatenate([-sine, cosine], axis=1),
            ],
            axis=0,
        )
        for cosine, sine in zip(part_of(3, 4), part_of(4, 5))
    ]
    row_inv = part_of(5, 6, 2 * PATCH)

    for step in steps:

        @pl.when(there((-step[0], -step[1])))
        def _():
            for n, message in enumerate(messages):
                if message[0] == step:
                    halo_copy(n).wait_recv()

    tall = rows + 2 * halo
    wide = lax.broadcasted_iota(jnp.int32, (tall, LANES), 1)
    in_l = (wide >= cells_c) & (wide < cells_c + MARGIN)
    in_r = (wide >= cells_c + MARGIN) & (wide < cells_c + 2 * MARGIN)
    got_l, got_r = side_l[...], side_r[...]

    def whole(p):
        left = pltpu.roll(got_l, (cells_c - p * MARGIN) % LANES, 1)
        right = pltpu.roll(got_r, (cells_c + MARGIN - p * MARGIN) % LANES, 1)
        return jnp.where(in_l, left, jnp.where(in_r, right, planes[p]))

    def lane_tiles(x):
        return [x[:, i : i + LANES] for i in range(0, x.shape[1], LANES)]

    fields = [jnp.concatenate([whole(2 * p), whole(2 * p + 1)], axis=0) for p in range(6)]
    outs = lane_tiles(dot(row_fwd, split(jnp.concatenate(fields, axis=1))))
    spectra = [jnp.concatenate([o[:PATCH], o[PATCH : 2 * PATCH]], axis=1) for o in outs]
    boxes = [o[2 * PATCH :] for o in outs]
    high, low = split(jnp.concatenate([whole(p) for p in range(12, 18)], axis=1))
    boxes += lane_tiles(mul(box_r, high) + mul(box_r, low))
    box = dot_exact(jnp.concatenate(boxes, axis=0), box_c) * (1.0 / 9.0)
    base = 12 * cells_r
    power = [box[base + i * cells_r : base + (i + 1) * cells_r] for i in range(6)]
    for k in range(2):
        for l in range(3):
            second = jnp.where(first[k][l], power[k + l + 1], power[k + l + 2])
            factor = lax.rsqrt(power[k] * second + 1e-06)
            for part in range(2):
                at = ((k * 3 + l) * 2 + part) * cells_r
                coh_ref[k, l, part] = (box[at : at + cells_r] * factor)[:, :cells_c]

    z = dot(split(jnp.concatenate(spectra, axis=0)), col_fwd)
    z_r, z_i = z[:, :LANES], z[:, LANES:]
    energy = z_r * z_r + z_i * z_i
    lane32 = lax.rem(lax.broadcasted_iota(jnp.int32, (6 * PATCH, LANES), 1), PATCH)
    left = jnp.where(lane32 == 0, pltpu.roll(energy, LANES - PATCH + 1, 1), pltpu.roll(energy, 1, 1))
    right = jnp.where(
        lane32 == PATCH - 1, pltpu.roll(energy, PATCH - 1, 1), pltpu.roll(energy, LANES - 1, 1)
    )
    across = energy + left + right

    def per_patch(values):
        sums = [
            jnp.sum(values[p * PATCH : (p + 1) * PATCH], axis=0, keepdims=True) for p in range(6)
        ]
        sums += [jnp.zeros((2, LANES), jnp.float32)]
        return dot_exact(jnp.concatenate(sums, axis=0), group) * (1.0 / (PATCH * PATCH))

    level = per_patch(energy)
    weights = []
    for p in range(6):
        part = across[p * PATCH : (p + 1) * PATCH]
        smooth = (part + pltpu.roll(part, 1, 0) + pltpu.roll(part, PATCH - 1, 0)) * (1.0 / 9.0)
        weights.append(jnp.sqrt(jnp.sqrt(smooth + level[p : p + 1] + 1e-06)))
    scale = 1.0 / per_patch(jnp.concatenate(weights, axis=0))
    filtered = []
    for p in range(6):
        weight = weights[p] * scale[p : p + 1]
        at = slice(p * PATCH, (p + 1) * PATCH)
        filtered.append(jnp.concatenate([z_r[at] * weight, z_i[at] * weight], axis=0))
    outs = lane_tiles(dot(row_inv, split(jnp.concatenate(filtered, axis=1))))
    back = [jnp.concatenate([o[:KEEP], o[KEEP:]], axis=1) for o in outs]
    final = dot(split(jnp.concatenate(back, axis=0)), col_inv)
    for p in range(6):
        at = slice(p * KEEP, (p + 1) * KEEP)
        filt_ref[p // 3, p % 3, 0] = final[at, :cells_c]
        filt_ref[p // 3, p % 3, 1] = final[at, LANES : LANES + cells_c]

    for c in range(chunks):
        far_copy(c).wait_send()
        near_copy(c, img_hbm).wait_send()
    for step in steps:

        @pl.when(there(step))
        def _():
            for n, message in enumerate(messages):
                if message[0] == step:
                    halo_copy(n).wait_send()


def body(images, secondaries):
    per_device, _, rows, cols = images.shape
    links = secondaries.shape[1]
    dates = lax.axis_size("date")
    assert per_device == 2 and links == 3 and rows == 2 * KEEP and dates % 2 == 0 and dates > 4
    cells_r, cells_c = rows // LOOK_R, cols // LOOK_C
    tall = rows + 2 * MARGIN * LOOK_R
    chunks = rows // BAND
    out = jax.ShapeDtypeStruct((per_device, links, 2, cells_r, cells_c), jnp.float32)
    table, starts = tables(rows, cols)
    vmem = pl.BlockSpec(memory_space=pltpu.VMEM)
    hbm = pl.BlockSpec(memory_space=pltpu.HBM)
    sizes = (dates, lax.axis_size("row"), lax.axis_size("col"))
    dma = pltpu.SemaphoreType.DMA
    return pl.pallas_call(
        functools.partial(kernel, sizes, starts),
        out_shape=(out, out),
        in_specs=[pl.BlockSpec(memory_space=pltpu.SMEM), hbm, hbm],
        out_specs=(vmem, vmem),
        scratch_shapes=[
            pltpu.VMEM(images.shape, jnp.float32),
            pltpu.VMEM(table.shape, jnp.bfloat16),
            pltpu.VMEM(images.shape, jnp.float32),
            pltpu.VMEM(images.shape, jnp.float32),
            pltpu.VMEM((18, tall, LANES), jnp.float32),
            pltpu.VMEM((rows, LANES), jnp.float32),
            pltpu.VMEM((rows, LANES), jnp.float32),
            pltpu.VMEM((tall, LANES), jnp.float32),
            pltpu.VMEM((tall, LANES), jnp.float32),
            dma((chunks,)),
            dma((chunks,)),
            dma((chunks,)),
            dma((chunks,)),
            dma((6 + 2 * chunks,)),
            dma((6 + 2 * chunks,)),
            dma((2,)),
        ],
        compiler_params=pltpu.CompilerParams(
            collective_id=0, has_side_effects=True, vmem_limit_bytes=32 * 1024 * 1024
        ),
        cost_estimate=pl.CostEstimate(flops=10**9, bytes_accessed=10**6, transcendentals=0),
    )(secondaries, images, jnp.asarray(table))


def solution(mesh):
    in_specs = (P("date", None, "row", "col"), P("date", None))
    out_specs = (P("date", None, None, "row", "col"), P("date", None, None, "row", "col"))
    return jax.shard_map(body, mesh=mesh, in_specs=in_specs, out_specs=out_specs, check_vma=False)
```

time: 38.2 us -> 32 us (0.84)
  the two profiles are of different devices: /device:TPU:3 before, /device:TPU:2 now
where the time goes in v2:
time: 32 us; the launch traced here: 31.8 us
  Pallas kernels  27.1 us (85%)
  local copies, waits for them, and re-layouts  4.04 us (13%)
  between operations  0.65 us (2%)
    pallas_call x1, Pallas kernels, body(): pl.pallas_call(functools.partial(kernel, sizes, starts), out_shape=(out,...  27.1 us
    unnamed x8, local copies, waits for them, and re-layouts  4.04 us

profile of v2, /device:TPU:2, one launch (start us, length us, event | category | flops | bytes accessed | tf_op | source)
XLA Modules:
  0.0 31.8 jit_solution(17062677473944233847)
XLA Ops:
  0.6 0.0 copy-start
  0.6 1.1 %copy-done = f32[2,2,48,768]{3,2,1,0:T(8,128)S(1)} copy-done((f32[2,2,48,768]{3,2,1,0:T(8,128)S(1)}, f32[2,2,48,768]{3,2,1,0:T(8,128)}, u32[]{:S(2)}) %copy-start) | copy-done | bytes 589848
  1.7 0.0 copy-start.1
  1.7 0.7 %copy-done.1 = s32[2,3]{1,0:T(2,128)S(1)} copy-done((s32[2,3]{1,0:T(2,128)S(1)}, s32[2,3]{1,0:T(2,128)}, u32[]{:S(2)}) %copy-start.1) | copy-done | bytes 48
  2.4 0.0 copy-start.2
  2.4 1.0 %copy-done.2 = bf16[2,672,128]{2,1,0:T(8,128)(2,1)S(1)} copy-done((bf16[2,672,128]{2,1,0:T(8,128)(2,1)S(1)}, bf16[2,672,128]{2,1,0:T(8,128)(2,1)}, u32[]{:S(2)}) %copy-start.2) | copy-done | bytes 344088
  3.4 27.1 %shard_map.50 = (f32[2,3,2,24,96]{4,3,2,1,0:T(8,128)S(1)}, f32[2,3,2,24,96]{4,3,2,1,0:T(8,128)S(1)}) custom-call(s32[2,3]{1,0:T(2,128)S(1)} %copy-done.1, f32[2,2,48,768]{3,2,1,0:T(8,128)S(1)} %copy-done, bf16[2,672,128]{2,1,0:T(8,128)(2,1)S(1)} %copy-done.2), custom_call_target="tpu_custom_call" | custom-call | flops 1000000000 | bytes 1000000 | tf_op jit(solution)/shard_map/pallas_call | solution.py:427
  30.5 0.7 %copy.7 = f32[2,3,2,24,96]{4,3,2,1,0:T(8,128)} copy(f32[2,3,2,24,96]{4,3,2,1,0:T(8,128)S(1)} %get-tuple-element.4) | data formatting | bytes 221184
  31.1 0.7 %copy.8 = f32[2,3,2,24,96]{4,3,2,1,0:T(8,128)} copy(f32[2,3,2,24,96]{4,3,2,1,0:T(8,128)S(1)} %get-tuple-element.5) | data formatting | bytes 221184
Async XLA Ops:
  0.6 1.1 %copy-start = (f32[2,2,48,768]{3,2,1,0:T(8,128)S(1)}, f32[2,2,48,768]{3,2,1,0:T(8,128)}, u32[]{:S(2)}) copy-start(f32[2,2,48,768]{3,2,1,0:T(8,128)} %img_hbm.1) | copy-start | bytes 1769476
  1.7 0.7 %copy-start.1 = (s32[2,3]{1,0:T(2,128)S(1)}, s32[2,3]{1,0:T(2,128)}, u32[]{:S(2)}) copy-start(s32[2,3]{1,0:T(2,128)} %sec_ref.1) | copy-start | bytes 76
  2.4 1.0 %copy-start.2 = (bf16[2,672,128]{2,1,0:T(8,128)(2,1)S(1)}, bf16[2,672,128]{2,1,0:T(8,128)(2,1)}, u32[]{:S(2)}) copy-start(bf16[2,672,128]{2,1,0:T(8,128)(2,1)} %constant.2.clone.table_hbm) | copy-start | bytes 1032196

commit v3 on v2

--- a/solution.py
+++ b/solution.py
@@ -17,6 +17,8 @@
 MARGIN = 4
 LANES = 128
 BAND = 8
+PIECE = 256
+VMEM_BYTES = 64 * 1024 * 1024 - 64 * 1024
 MESH = pl.DeviceIdType.MESH
 
 
@@ -88,11 +90,12 @@
 def kernel(
     sizes,
     starts,
-    sec_ref,
+    sec_hbm,
     img_hbm,
     table_hbm,
     filt_ref,
     coh_ref,
+    sec_ref,
     img_ref,
     table,
     near,
@@ -132,6 +135,8 @@
     order = [0, chunks - 1] + list(range(1, chunks - 1))
     load_img = pltpu.make_async_copy(img_hbm, img_ref, local_sem.at[0])
     load_table = pltpu.make_async_copy(table_hbm, table, local_sem.at[1])
+    load_sec = pltpu.make_async_copy(sec_hbm, sec_ref, local_sem.at[2])
+    load_sec.start()
     load_img.start()
     load_table.start()
     barrier = pltpu.get_barrier_semaphore()
@@ -156,32 +161,37 @@
     def band(c):
         return pl.ds(c * BAND, BAND)
 
-    def far_copy(c):
+    pieces = cols // PIECE
+
+    def far_copy(c, h):
+        part = (slice(None), slice(None), band(c), pl.ds(h * PIECE, PIECE))
         return pltpu.make_async_remote_copy(
-            src_ref=img_hbm.at[:, :, band(c)],
-            dst_ref=far.at[:, :, band(c)],
-            send_sem=far_send.at[c],
-            recv_sem=far_recv.at[c],
+            src_ref=img_hbm.at[part],
+            dst_ref=far.at[part],
+            send_sem=far_send.at[c * pieces + h],
+            recv_sem=far_recv.at[c * pieces + h],
             device_id=(before, row, col),
             device_id_type=MESH,
         )
 
-    def near_copy(c, source):
+    def near_copy(c, h, source):
+        part = (slice(None), slice(None), band(c), pl.ds(h * PIECE, PIECE))
         return pltpu.make_async_remote_copy(
-            src_ref=source.at[:, :, band(c)],
-            dst_ref=near.at[:, :, band(c)],
-            send_sem=near_send.at[c],
-            recv_sem=near_recv.at[c],
+            src_ref=source.at[part],
+            dst_ref=near.at[part],
+            send_sem=near_send.at[c * pieces + h],
+            recv_sem=near_recv.at[c * pieces + h],
             device_id=(mate, row, col),
             device_id_type=MESH,
         )
 
     for c in order:
-        far_copy(c).start()
-
-        @pl.when(odd)
-        def _():
-            near_copy(c, img_hbm).start()
+        for h in range(pieces):
+            far_copy(c, h).start()
+
+            @pl.when(odd)
+            def _():
+                near_copy(c, h, img_hbm).start()
 
     for step in steps:
 
@@ -196,6 +206,7 @@
                 side[at] = jnp.zeros_like(side[at])
 
     total = 2 * dates
+    load_sec.wait()
 
     def is_first(k, l):
         return lax.rem(sec_ref[k, l] - (2 * date + k) + total, total) == l + 1
@@ -216,12 +227,12 @@
     box_c = jnp.where(box_c & (to_lane < cells_c), 1.0, 0.0).astype(jnp.bfloat16)
     group = jnp.where(from_lane // PATCH == to_lane // PATCH, 1.0, 0.0).astype(jnp.bfloat16)
 
-    def process(c):
-        at = band(c)
+    def look_sums(c, h):
+        at, across = band(c), pl.ds(h * PIECE, PIECE)
 
         def date_image(i):
             source = (img_ref, near, far)[i // 2]
-            return source[i % 2, 0, at], source[i % 2, 1, at]
+            return source[i % 2, 0, at, across], source[i % 2, 1, at, across]
 
         images = [date_image(i) for i in range(6)]
         parts = []
@@ -233,11 +244,14 @@
                 b_i = jnp.where(first[k][l], low[1], high[1])
                 parts += [a_r * b_r + a_i * b_i, a_i * b_r - a_r * b_i]
         parts += [r * r + i * i for r, i in images]
-        summed = dot_exact(jnp.concatenate(parts, axis=0), looks)
+        return dot_exact(jnp.concatenate(parts, axis=0), looks[h * PIECE : (h + 1) * PIECE])
+
+    def keep(c, summed):
+        at = band(c)
         lanes = lax.broadcasted_iota(jnp.int32, (BAND, LANES), 1)
         pack_l = jnp.zeros((BAND, LANES), jnp.float32)
         pack_r = jnp.zeros((BAND, LANES), jnp.float32)
-        for p in range(len(parts)):
+        for p in range(planes.shape[0]):
             own = summed[p * BAND : (p + 1) * BAND]
             planes[p, pl.ds(halo + c * BAND, BAND)] = own
             mine = (lanes >= p * MARGIN) & (lanes < (p + 1) * MARGIN)
@@ -276,14 +290,18 @@
 
     load_img.wait()
     for c in order:
-        far_copy(c).wait_recv()
-
-        @pl.when(jnp.logical_not(odd))
-        def _():
-            near_copy(c, far).start()
-
-        near_copy(c, img_hbm).wait_recv()
-        process(c)
+        summed = None
+        for h in range(pieces):
+            far_copy(c, h).wait_recv()
+
+            @pl.when(jnp.logical_not(odd))
+            def _():
+                near_copy(c, h, far).start()
+
+            near_copy(c, h, img_hbm).wait_recv()
+            part = look_sums(c, h)
+            summed = part if summed is None else summed + part
+        keep(c, summed)
         for step in steps:
 
             @pl.when(there(step))
@@ -399,8 +417,9 @@
         filt_ref[p // 3, p % 3, 1] = final[at, LANES : LANES + cells_c]
 
     for c in range(chunks):
-        far_copy(c).wait_send()
-        near_copy(c, img_hbm).wait_send()
+        for h in range(pieces):
+            far_copy(c, h).wait_send()
+            near_copy(c, h, img_hbm).wait_send()
     for step in steps:
 
         @pl.when(there(step))
@@ -427,9 +446,10 @@
     return pl.pallas_call(
         functools.partial(kernel, sizes, starts),
         out_shape=(out, out),
-        in_specs=[pl.BlockSpec(memory_space=pltpu.SMEM), hbm, hbm],
+        in_specs=[hbm, hbm, hbm],
         out_specs=(vmem, vmem),
         scratch_shapes=[
+            pltpu.SMEM(secondaries.shape, jnp.int32),
             pltpu.VMEM(images.shape, jnp.float32),
             pltpu.VMEM(table.shape, jnp.bfloat16),
             pltpu.VMEM(images.shape, jnp.float32),
@@ -439,16 +459,16 @@
             pltpu.VMEM((rows, LANES), jnp.float32),
             pltpu.VMEM((tall, LANES), jnp.float32),
             pltpu.VMEM((tall, LANES), jnp.float32),
-            dma((chunks,)),
-            dma((chunks,)),
-            dma((chunks,)),
-            dma((chunks,)),
+            dma((chunks * (cols // PIECE),)),
+            dma((chunks * (cols // PIECE),)),
+            dma((chunks * (cols // PIECE),)),
+            dma((chunks * (cols // PIECE),)),
             dma((6 + 2 * chunks,)),
             dma((6 + 2 * chunks,)),
-            dma((2,)),
+            dma((3,)),
         ],
         compiler_params=pltpu.CompilerParams(
-            collective_id=0, has_side_effects=True, vmem_limit_bytes=32 * 1024 * 1024
+            collective_id=0, has_side_effects=True, vmem_limit_bytes=VMEM_BYTES
         ),
         cost_estimate=pl.CostEstimate(flops=10**9, bytes_accessed=10**6, transcendentals=0),
     )(secondaries, images, jnp.asarray(table))

time: 32 us -> 30.6 us (0.956)
  local copies, waits for them, and re-layouts: 4.04 us -> 2.28 us
  Pallas kernels: 27.1 us -> 27.5 us
    unnamed x8 -> x4, local copies, waits for them, and re-layouts: 4.04 us -> 2.28 us
    pallas_call x1, Pallas kernels: 27.1 us -> 27.5 us  [body(): pl.pallas_call(functools.partial(kernel, sizes, starts), out_shape=(out,...]
where the time goes in v3:
time: 30.6 us; the launch traced here: 30.5 us
  Pallas kernels  27.5 us (90%)
  local copies, waits for them, and re-layouts  2.28 us (7%)
  between operations  0.65 us (2%)
    pallas_call x1, Pallas kernels, body(): pl.pallas_call(functools.partial(kernel, sizes, starts), out_shape=(out,...  27.5 us
    unnamed x4, local copies, waits for them, and re-layouts  2.28 us

profile of v3, /device:TPU:2, one launch (start us, length us, event | category | flops | bytes accessed | tf_op | source)
XLA Modules:
  0.0 30.5 jit_solution(7453040945377407979)
XLA Ops:
  0.6 27.5 %shard_map.50 = (f32[2,3,2,24,96]{4,3,2,1,0:T(8,128)}, f32[2,3,2,24,96]{4,3,2,1,0:T(8,128)}) custom-call(s32[2,3]{1,0:T(2,128)} %sec_hbm.1, f32[2,2,48,768]{3,2,1,0:T(8,128)} %img_hbm.1, bf16[2,672,128]{2,1,0:T(8,128)(2,1)} %constant.2.clone.table_hbm), custom_call_target="tpu_custom_call" | custom-call | flops 1000000000 | bytes 1000000 | tf_op jit(solution)/shard_map/pallas_call | solution.py:446
  28.2 0.0 copy-start
  28.2 1.6 %copy.7 = f32[2,3,2,24,96]{4,3,2,1,0:T(8,128)} copy(f32[2,3,2,24,96]{4,3,2,1,0:T(8,128)} %get-tuple-element.4) | data formatting | bytes 221184
  29.8 0.0 copy-done
  29.8 0.7 %copy.8 = f32[2,3,2,24,96]{4,3,2,1,0:T(8,128)} copy(f32[2,3,2,24,96]{4,3,2,1,0:T(8,128)S(1)} %copy-done) | data formatting | bytes 221184
Async XLA Ops:
  28.2 1.6 %copy-start = (f32[2,3,2,24,96]{4,3,2,1,0:T(8,128)S(1)}, f32[2,3,2,24,96]{4,3,2,1,0:T(8,128)}, u32[]{:S(2)}) copy-start(f32[2,3,2,24,96]{4,3,2,1,0:T(8,128)} %get-tuple-element.5) | copy-start | bytes 331780

commit v4 on v3

--- a/solution.py
+++ b/solution.py
@@ -18,7 +18,7 @@
 LANES = 128
 BAND = 8
 PIECE = 256
-VMEM_BYTES = 64 * 1024 * 1024 - 64 * 1024
+VMEM_BYTES = 64 * 1024 * 1024 - 800 * 1024
 MESH = pl.DeviceIdType.MESH
 
 
@@ -340,34 +340,49 @@
     ]
     row_inv = part_of(5, 6, 2 * PATCH)
 
-    for step in steps:
-
-        @pl.when(there((-step[0], -step[1])))
-        def _():
-            for n, message in enumerate(messages):
-                if message[0] == step:
-                    halo_copy(n).wait_recv()
+    def wait_halo(sides):
+        for step in steps:
+            if (step[1] != 0) != sides:
+                continue
+
+            @pl.when(there((-step[0], -step[1])))
+            def _():
+                for n, message in enumerate(messages):
+                    if message[0] == step:
+                        halo_copy(n).wait_recv()
+
+    def lane_tiles(x):
+        return [x[:, i : i + LANES] for i in range(0, x.shape[1], LANES)]
+
+    wait_halo(False)
+    fields = [jnp.concatenate([planes[2 * p], planes[2 * p + 1]], axis=0) for p in range(6)]
+    outs = lane_tiles(dot(row_fwd, split(jnp.concatenate(fields, axis=1))))
+    high, low = split(jnp.concatenate([planes[p] for p in range(12, 18)], axis=1))
+    outs += lane_tiles(mul(box_r, high) + mul(box_r, low))
+    wait_halo(True)
 
     tall = rows + 2 * halo
     wide = lax.broadcasted_iota(jnp.int32, (tall, LANES), 1)
-    in_l = (wide >= cells_c) & (wide < cells_c + MARGIN)
-    in_r = (wide >= cells_c + MARGIN) & (wide < cells_c + 2 * MARGIN)
+    in_left = lax.rem(wide, 2 * MARGIN) < MARGIN
     got_l, got_r = side_l[...], side_r[...]
-
-    def whole(p):
-        left = pltpu.roll(got_l, (cells_c - p * MARGIN) % LANES, 1)
-        right = pltpu.roll(got_r, (cells_c + MARGIN - p * MARGIN) % LANES, 1)
-        return jnp.where(in_l, left, jnp.where(in_r, right, planes[p]))
-
-    def lane_tiles(x):
-        return [x[:, i : i + LANES] for i in range(0, x.shape[1], LANES)]
-
-    fields = [jnp.concatenate([whole(2 * p), whole(2 * p + 1)], axis=0) for p in range(6)]
-    outs = lane_tiles(dot(row_fwd, split(jnp.concatenate(fields, axis=1))))
-    spectra = [jnp.concatenate([o[:PATCH], o[PATCH : 2 * PATCH]], axis=1) for o in outs]
-    boxes = [o[2 * PATCH :] for o in outs]
-    high, low = split(jnp.concatenate([whole(p) for p in range(12, 18)], axis=1))
-    boxes += lane_tiles(mul(box_r, high) + mul(box_r, low))
+    even = jnp.where(in_left, got_l, pltpu.roll(got_r, MARGIN, 1))
+    later = jnp.where(in_left, pltpu.roll(got_l, LANES - MARGIN, 1), got_r)
+    margins = dot(row_fwd, split(jnp.concatenate([even, later], axis=0)))
+
+    def with_margins(out, q, at):
+        moved = pltpu.roll(margins[at], (cells_c - 2 * MARGIN * q) % LANES, 1)
+        lanes = lax.broadcasted_iota(jnp.int32, out.shape, 1)
+        return jnp.where((lanes >= cells_c) & (lanes < cells_c + 2 * MARGIN), moved, out)
+
+    middle = 2 * PATCH
+    spectra, boxes = [], []
+    for p in range(6):
+        out = with_margins(outs[p], p, slice(None))
+        spectra.append(jnp.concatenate([out[:PATCH], out[PATCH:middle]], axis=1))
+        boxes.append(out[middle:])
+    for i in range(6):
+        start = middle + (i % 2) * cells_r
+        boxes.append(with_margins(outs[6 + i], 6 + i // 2, slice(start, start + cells_r)))
     box = dot_exact(jnp.concatenate(boxes, axis=0), box_c) * (1.0 / 9.0)
     base = 12 * cells_r
     power = [box[base + i * cells_r : base + (i + 1) * cells_r] for i in range(6)]
@@ -429,6 +444,17 @@
                     halo_copy(n).wait_send()
 
 
+def write(filt_in, coh_in, filt_out, coh_out, sems):
+    copies = [
+        pltpu.make_async_copy(filt_in, filt_out, sems.at[0]),
+        pltpu.make_async_copy(coh_in, coh_out, sems.at[1]),
+    ]
+    for copy in copies:
+        copy.start()
+    for copy in copies:
+        copy.wait()
+
+
 def body(images, secondaries):
     per_device, _, rows, cols = images.shape
     links = secondaries.shape[1]
@@ -443,9 +469,9 @@
     hbm = pl.BlockSpec(memory_space=pltpu.HBM)
     sizes = (dates, lax.axis_size("row"), lax.axis_size("col"))
     dma = pltpu.SemaphoreType.DMA
-    return pl.pallas_call(
+    results = pl.pallas_call(
         functools.partial(kernel, sizes, starts),
-        out_shape=(out, out),
+        out_shape=(pltpu.VMEM(out.shape, out.dtype),) * 2,
         in_specs=[hbm, hbm, hbm],
         out_specs=(vmem, vmem),
         scratch_shapes=[
@@ -472,6 +498,14 @@
         ),
         cost_estimate=pl.CostEstimate(flops=10**9, bytes_accessed=10**6, transcendentals=0),
     )(secondaries, images, jnp.asarray(table))
+    return pl.pallas_call(
+        write,
+        out_shape=(out, out),
+        in_specs=[vmem, vmem],
+        out_specs=(hbm, hbm),
+        scratch_shapes=[dma((2,))],
+        compiler_params=pltpu.CompilerParams(vmem_limit_bytes=1024 * 1024),
+    )(*results)
 
 
 def solution(mesh):

time: 30.6 us -> 28.2 us (0.922)
  local copies, waits for them, and re-layouts: 2.28 us -> 0 us
    unnamed x4 -> x0, local copies, waits for them, and re-layouts: 2.28 us -> none
    pallas_call x1 -> x2, Pallas kernels: 27.5 us -> 27.4 us  [the longest x1 26.7 us: body(): pl.pallas_call(functools.partial(kernel, sizes, starts), out_shape=(pltpu...]
where the time goes in v4:
time: 28.2 us; the launch traced here: 28 us
  Pallas kernels  27.4 us (97%)
  between operations  0.64 us (2%)
    pallas_call x1, Pallas kernels, body(): pl.pallas_call(functools.partial(kernel, sizes, starts), out_shape=(pltpu...  26.7 us
    pallas_call x1, Pallas kernels, body(): pl.pallas_call(write, out_shape=(out, out), in_specs=[vmem, vmem], out_sp...  0.73 us

profile of v4, /device:TPU:2, one launch (start us, length us, event | category | flops | bytes accessed | tf_op | source)
XLA Modules:
  0.0 28.0 jit_solution(2431965905237991861)
XLA Ops:
  0.6 26.7 %shard_map.50 = (f32[2,3,2,24,96]{4,3,2,1,0:T(8,128)S(1)}, f32[2,3,2,24,96]{4,3,2,1,0:T(8,128)S(1)}) custom-call(s32[2,3]{1,0:T(2,128)} %sec_hbm.1, f32[2,2,48,768]{3,2,1,0:T(8,128)} %img_hbm.1, bf16[2,672,128]{2,1,0:T(8,128)(2,1)} %constant.2.clone.table_hbm), custom_call_target="tpu_custom_call" | custom-call | flops 1000000000 | bytes 1000000 | tf_op jit(solution)/shard_map/pallas_call | solution.py:472
  27.3 0.7 %shard_map.51 = (f32[2,3,2,24,96]{4,3,2,1,0:T(8,128)}, f32[2,3,2,24,96]{4,3,2,1,0:T(8,128)}) custom-call(f32[2,3,2,24,96]{4,3,2,1,0:T(8,128)S(1)} %get-tuple-element.4.filt_in, f32[2,3,2,24,96]{4,3,2,1,0:T(8,128)S(1)} %get-tuple-element.5.coh_in), custom_call_target="tpu_custom_call" | custom-call | tf_op jit(solution)/shard_map/pallas_call | solution.py:501

commit v5 on v4

--- a/solution.py
+++ b/solution.py
@@ -18,6 +18,7 @@
 LANES = 128
 BAND = 8
 PIECE = 256
+DIRECT = 2
 VMEM_BYTES = 64 * 1024 * 1024 - 800 * 1024
 MESH = pl.DeviceIdType.MESH
 
@@ -122,6 +123,7 @@
     date, row, col = lax.axis_index("date"), lax.axis_index("row"), lax.axis_index("col")
     odd = lax.rem(date, 2) == 1
     mate = date + 1 - 2 * lax.rem(date, 2)
+    cross = lax.rem(date + dates - 1 + 2 * lax.rem(date, 2), dates)
     before = lax.rem(date + dates - 2, dates)
     after = lax.rem(date + 2, dates)
     steps = [(r, c) for r in (-1, 0, 1) for c in (-1, 0, 1) if (r, c) != (0, 0)]
@@ -140,9 +142,9 @@
     load_img.start()
     load_table.start()
     barrier = pltpu.get_barrier_semaphore()
-    for other in (before, after, mate):
+    for other in (before, after, mate, cross):
         pl.semaphore_signal(barrier, inc=1, device_id=(other, row, col), device_id_type=MESH)
-    count = jnp.int32(3)
+    count = jnp.int32(4)
     for step in steps:
         here = there(step)
 
@@ -174,16 +176,24 @@
             device_id_type=MESH,
         )
 
-    def near_copy(c, h, source):
+    def near_copy(c, h, source, target=mate):
         part = (slice(None), slice(None), band(c), pl.ds(h * PIECE, PIECE))
         return pltpu.make_async_remote_copy(
             src_ref=source.at[part],
             dst_ref=near.at[part],
             send_sem=near_send.at[c * pieces + h],
             recv_sem=near_recv.at[c * pieces + h],
-            device_id=(mate, row, col),
+            device_id=(target, row, col),
             device_id_type=MESH,
         )
+
+    every = [(c, h) for c in order for h in range(pieces)]
+    direct = every[len(every) - DIRECT :]
+    for c, h in direct:
+
+        @pl.when(jnp.logical_not(odd))
+        def _():
+            near_copy(c, h, img_hbm, cross).start()
 
     for c in order:
         for h in range(pieces):
@@ -294,9 +304,11 @@
         for h in range(pieces):
             far_copy(c, h).wait_recv()
 
-            @pl.when(jnp.logical_not(odd))
-            def _():
-                near_copy(c, h, far).start()
+            if (c, h) not in direct:
+
+                @pl.when(jnp.logical_not(odd))
+                def _():
+                    near_copy(c, h, far).start()
 
             near_copy(c, h, img_hbm).wait_recv()
             part = look_sums(c, h)

time: 28.2 us -> 29 us (1.028)
  the two profiles are of different devices: /device:TPU:2 before, /device:TPU:26 now
where the time goes in v5:
time: 29 us; the launch traced here: 28.9 us
  Pallas kernels  28.2 us (97%)
  between operations  0.64 us (2%)
    pallas_call x1, Pallas kernels, body(): pl.pallas_call(functools.partial(kernel, sizes, starts), out_shape=(pltpu...  27.5 us
    pallas_call x1, Pallas kernels, body(): pl.pallas_call(write, out_shape=(out, out), in_specs=[vmem, vmem], out_sp...  0.73 us

profile of v5, /device:TPU:26, one launch (start us, length us, event | category | flops | bytes accessed | tf_op | source)
XLA Modules:
  0.0 28.9 jit_solution(4862472409613686609)
XLA Ops:
  0.6 27.5 %shard_map.50 = (f32[2,3,2,24,96]{4,3,2,1,0:T(8,128)S(1)}, f32[2,3,2,24,96]{4,3,2,1,0:T(8,128)S(1)}) custom-call(s32[2,3]{1,0:T(2,128)} %sec_hbm.1, f32[2,2,48,768]{3,2,1,0:T(8,128)} %img_hbm.1, bf16[2,672,128]{2,1,0:T(8,128)(2,1)} %constant.2.clone.table_hbm), custom_call_target="tpu_custom_call" | custom-call | flops 1000000000 | bytes 1000000 | tf_op jit(solution)/shard_map/pallas_call | solution.py:484
  28.1 0.7 %shard_map.51 = (f32[2,3,2,24,96]{4,3,2,1,0:T(8,128)}, f32[2,3,2,24,96]{4,3,2,1,0:T(8,128)}) custom-call(f32[2,3,2,24,96]{4,3,2,1,0:T(8,128)S(1)} %get-tuple-element.4.filt_in, f32[2,3,2,24,96]{4,3,2,1,0:T(8,128)S(1)} %get-tuple-element.5.coh_in), custom_call_target="tpu_custom_call" | custom-call | tf_op jit(solution)/shard_map/pallas_call | solution.py:513

commit v6 on v4

--- a/solution.py
+++ b/solution.py
@@ -60,7 +60,7 @@
         inv_c[b * PATCH : (b + 1) * PATCH, b * KEEP : (b + 1) * KEEP] = cosine[:, centre]
         inv_s[b * PATCH : (b + 1) * PATCH, b * KEEP : (b + 1) * KEEP] = sine[:, centre]
     scale = 1.0 / (PATCH * PATCH)
-    row_inv = np.pad(row_inv, ((0, 0), (0, LANES - 2 * PATCH)))
+    row_inv = np.concatenate([row_inv, row_inv], axis=1)
     stacked = [row_fwd, col_c, col_s, inv_c * scale, inv_s * scale, row_inv]
     whole = np.concatenate(stacked, axis=0).astype(np.float32)
     high = whole.astype(ml_dtypes.bfloat16)
@@ -85,6 +85,15 @@
 def dot_exact(x, b):
     high, low = split(x)
     return mul(high, b) + mul(low, b)
+
+
+def dot_rows(twice, low_table, x):
+    high, low = split(x)
+    return mul(twice, jnp.concatenate([high, low], axis=0)) + mul(low_table, high)
+
+
+def dot_twice(x, twice):
+    return mul(jnp.concatenate(split(x), axis=1), twice)
 
 
 def kernel(
@@ -225,6 +234,15 @@
     box_c = (from_lane == to_lane) | (from_lane == lane_of(to_lane - 1))
     box_c = box_c | (from_lane == lane_of(to_lane + 1))
     box_c = jnp.where(box_c & (to_lane < cells_c), 1.0, 0.0).astype(jnp.bfloat16)
+    box_c = jnp.concatenate([box_c, box_c], axis=0)
+    from_cell = jnp.where(
+        from_lane < cells_c,
+        from_lane,
+        jnp.where(from_lane < cells_c + MARGIN, from_lane - cells_c, from_lane) - MARGIN,
+    )
+    in_patch = from_cell - (to_lane // PATCH * KEEP - MARGIN)
+    window = (in_patch >= 0) & (in_patch < PATCH) & (from_lane < cells_c + 2 * MARGIN)
+    window = jnp.where(window, 1.0, 0.0).astype(jnp.bfloat16)
     group = jnp.where(from_lane // PATCH == to_lane // PATCH, 1.0, 0.0).astype(jnp.bfloat16)
 
     def look_sums(c, h):
@@ -316,7 +334,8 @@
         rows_at = slice(starts[i], starts[j])
         return table[0, rows_at, :lanes], table[1, rows_at, :lanes]
 
-    row_fwd = part_of(0, 1)
+    row_fwd, row_fwd_low = part_of(0, 1)
+    row_fwd = jnp.concatenate([row_fwd, row_fwd], axis=1)
     box_r = table[0, starts[0] + 2 * PATCH : starts[0] + 2 * PATCH + cells_r, : rows + 2 * halo]
     col_fwd = [
         jnp.concatenate(
@@ -338,7 +357,8 @@
         )
         for cosine, sine in zip(part_of(3, 4), part_of(4, 5))
     ]
-    row_inv = part_of(5, 6, 2 * PATCH)
+    row_inv = table[0, starts[5] : starts[6]]
+    row_inv_low = table[1, starts[5] : starts[6], : 2 * PATCH]
 
     def wait_halo(sides):
         for step in steps:
@@ -356,9 +376,10 @@
 
     wait_halo(False)
     fields = [jnp.concatenate([planes[2 * p], planes[2 * p + 1]], axis=0) for p in range(6)]
-    outs = lane_tiles(dot(row_fwd, split(jnp.concatenate(fields, axis=1))))
-    high, low = split(jnp.concatenate([planes[p] for p in range(12, 18)], axis=1))
-    outs += lane_tiles(mul(box_r, high) + mul(box_r, low))
+    outs = lane_tiles(dot_rows(row_fwd, row_fwd_low, jnp.concatenate(fields, axis=1)))
+    powers = jnp.concatenate([planes[p] for p in range(12, 18)], axis=1)
+    box_twice = jnp.concatenate([box_r, box_r], axis=1)
+    outs += lane_tiles(mul(box_twice, jnp.concatenate(split(powers), axis=0)))
     wait_halo(True)
 
     tall = rows + 2 * halo
@@ -367,7 +388,7 @@
     got_l, got_r = side_l[...], side_r[...]
     even = jnp.where(in_left, got_l, pltpu.roll(got_r, MARGIN, 1))
     later = jnp.where(in_left, pltpu.roll(got_l, LANES - MARGIN, 1), got_r)
-    margins = dot(row_fwd, split(jnp.concatenate([even, later], axis=0)))
+    margins = dot_rows(row_fwd, row_fwd_low, jnp.concatenate([even, later], axis=0))
 
     def with_margins(out, q, at):
         moved = pltpu.roll(margins[at], (cells_c - 2 * MARGIN * q) % LANES, 1)
@@ -383,7 +404,7 @@
     for i in range(6):
         start = middle + (i % 2) * cells_r
         boxes.append(with_margins(outs[6 + i], 6 + i // 2, slice(start, start + cells_r)))
-    box = dot_exact(jnp.concatenate(boxes, axis=0), box_c) * (1.0 / 9.0)
+    box = dot_twice(jnp.concatenate(boxes, axis=0), box_c) * (1.0 / 9.0)
     base = 12 * cells_r
     power = [box[base + i * cells_r : base + (i + 1) * cells_r] for i in range(6)]
     for k in range(2):
@@ -404,26 +425,29 @@
     )
     across = energy + left + right
 
-    def per_patch(values):
-        sums = [
-            jnp.sum(values[p * PATCH : (p + 1) * PATCH], axis=0, keepdims=True) for p in range(6)
-        ]
+    def per_patch(tiles, sums_of, scale):
+        sums = [jnp.sum(tile, axis=0, keepdims=True) for tile in tiles]
         sums += [jnp.zeros((2, LANES), jnp.float32)]
-        return dot_exact(jnp.concatenate(sums, axis=0), group) * (1.0 / (PATCH * PATCH))
-
-    level = per_patch(energy)
+        return dot_exact(jnp.concatenate(sums, axis=0), sums_of) * scale
+
+    level = per_patch(
+        [s[:, :LANES] * s[:, :LANES] + s[:, LANES:] * s[:, LANES:] for s in spectra],
+        window,
+        1.0 / PATCH,
+    )
     weights = []
     for p in range(6):
         part = across[p * PATCH : (p + 1) * PATCH]
         smooth = (part + pltpu.roll(part, 1, 0) + pltpu.roll(part, PATCH - 1, 0)) * (1.0 / 9.0)
         weights.append(jnp.sqrt(jnp.sqrt(smooth + level[p : p + 1] + 1e-06)))
-    scale = 1.0 / per_patch(jnp.concatenate(weights, axis=0))
+    scale = 1.0 / per_patch(weights, group, 1.0 / (PATCH * PATCH))
     filtered = []
     for p in range(6):
-        weight = weights[p] * scale[p : p + 1]
+        weight = weights[p]
         at = slice(p * PATCH, (p + 1) * PATCH)
         filtered.append(jnp.concatenate([z_r[at] * weight, z_i[at] * weight], axis=0))
-    outs = lane_tiles(dot(row_inv, split(jnp.concatenate(filtered, axis=1))))
+    outs = lane_tiles(dot_rows(row_inv, row_inv_low, jnp.concatenate(filtered, axis=1)))
+    outs = [o * scale[p : p + 1] for p, o in enumerate(outs)]
     back = [jnp.concatenate([o[:KEEP], o[KEEP:]], axis=1) for o in outs]
     final = dot(split(jnp.concatenate(back, axis=0)), col_inv)
     for p in range(6):

time: 28.2 us -> 27.9 us (0.989)
  Pallas kernels: 27.4 us -> 27.1 us
    pallas_call x1, Pallas kernels: 26.7 us -> 26.4 us  [body(): pl.pallas_call(functools.partial(kernel, sizes, starts), out_shape=(pltpu...]
where the time goes in v6:
time: 27.9 us; the launch traced here: 27.7 us
  Pallas kernels  27.1 us (97%)
  between operations  0.64 us (2%)
    pallas_call x1, Pallas kernels, body(): pl.pallas_call(functools.partial(kernel, sizes, starts), out_shape=(pltpu...  26.4 us
    pallas_call x1, Pallas kernels, body(): pl.pallas_call(write, out_shape=(out, out), in_specs=[vmem, vmem], out_sp...  0.73 us

profile of v6, /device:TPU:2, one launch (start us, length us, event | category | flops | bytes accessed | tf_op | source)
XLA Modules:
  0.0 27.7 jit_solution(4500877050719946211)
XLA Ops:
  0.6 26.4 %shard_map.50 = (f32[2,3,2,24,96]{4,3,2,1,0:T(8,128)S(1)}, f32[2,3,2,24,96]{4,3,2,1,0:T(8,128)S(1)}) custom-call(s32[2,3]{1,0:T(2,128)} %sec_hbm.1, f32[2,2,48,768]{3,2,1,0:T(8,128)} %img_hbm.1, bf16[2,672,128]{2,1,0:T(8,128)(2,1)} %constant.2.clone.table_hbm), custom_call_target="tpu_custom_call" | custom-call | flops 1000000000 | bytes 1000000 | tf_op jit(solution)/shard_map/pallas_call | solution.py:496
  27.0 0.7 %shard_map.51 = (f32[2,3,2,24,96]{4,3,2,1,0:T(8,128)}, f32[2,3,2,24,96]{4,3,2,1,0:T(8,128)}) custom-call(f32[2,3,2,24,96]{4,3,2,1,0:T(8,128)S(1)} %get-tuple-element.4.filt_in, f32[2,3,2,24,96]{4,3,2,1,0:T(8,128)S(1)} %get-tuple-element.5.coh_in), custom_call_target="tpu_custom_call" | custom-call | tf_op jit(solution)/shard_map/pallas_call | solution.py:525

commit v7 on v6

--- a/solution.py
+++ b/solution.py
@@ -307,18 +307,24 @@
         )
 
     load_img.wait()
-    for c in order:
-        summed = None
-        for h in range(pieces):
-            far_copy(c, h).wait_recv()
+    every = [(c, h) for c in order for h in range(pieces)]
+    summed = None
+    for now, done in zip(every + [None], [None] + every):
+        if now is not None:
+            far_copy(*now).wait_recv()
 
             @pl.when(jnp.logical_not(odd))
             def _():
-                near_copy(c, h, far).start()
-
-            near_copy(c, h, img_hbm).wait_recv()
-            part = look_sums(c, h)
-            summed = part if summed is None else summed + part
+                near_copy(*now, far).start()
+
+        if done is None:
+            continue
+        c, h = done
+        near_copy(c, h, img_hbm).wait_recv()
+        part = look_sums(c, h)
+        summed = part if h == 0 else summed + part
+        if h < pieces - 1:
+            continue
         keep(c, summed)
         for step in steps:
 

time: 27.9 us -> 27.5 us (0.986)
  Pallas kernels: 27.1 us -> 26.8 us
    pallas_call x1, Pallas kernels: 26.4 us -> 26 us  [body(): pl.pallas_call(functools.partial(kernel, sizes, starts), out_shape=(pltpu...]
where the time goes in v7:
time: 27.5 us; the launch traced here: 27.4 us
  Pallas kernels  26.8 us (97%)
  between operations  0.64 us (2%)
    pallas_call x1, Pallas kernels, body(): pl.pallas_call(functools.partial(kernel, sizes, starts), out_shape=(pltpu...  26 us
    pallas_call x1, Pallas kernels, body(): pl.pallas_call(write, out_shape=(out, out), in_specs=[vmem, vmem], out_sp...  0.73 us

profile of v7, /device:TPU:2, one launch (start us, length us, event | category | flops | bytes accessed | tf_op | source)
XLA Modules:
  0.0 27.4 jit_solution(2264578349819542687)
XLA Ops:
  0.6 26.0 %shard_map.50 = (f32[2,3,2,24,96]{4,3,2,1,0:T(8,128)S(1)}, f32[2,3,2,24,96]{4,3,2,1,0:T(8,128)S(1)}) custom-call(s32[2,3]{1,0:T(2,128)} %sec_hbm.1, f32[2,2,48,768]{3,2,1,0:T(8,128)} %img_hbm.1, bf16[2,672,128]{2,1,0:T(8,128)(2,1)} %constant.2.clone.table_hbm), custom_call_target="tpu_custom_call" | custom-call | flops 1000000000 | bytes 1000000 | tf_op jit(solution)/shard_map/pallas_call | solution.py:502
  26.7 0.7 %shard_map.51 = (f32[2,3,2,24,96]{4,3,2,1,0:T(8,128)}, f32[2,3,2,24,96]{4,3,2,1,0:T(8,128)}) custom-call(f32[2,3,2,24,96]{4,3,2,1,0:T(8,128)S(1)} %get-tuple-element.4.filt_in, f32[2,3,2,24,96]{4,3,2,1,0:T(8,128)S(1)} %get-tuple-element.5.coh_in), custom_call_target="tpu_custom_call" | custom-call | tf_op jit(solution)/shard_map/pallas_call | solution.py:531

commit v8 on v7

--- a/solution.py
+++ b/solution.py
@@ -18,6 +18,7 @@
 LANES = 128
 BAND = 8
 PIECE = 256
+DIRECT = 2
 VMEM_BYTES = 64 * 1024 * 1024 - 800 * 1024
 MESH = pl.DeviceIdType.MESH
 
@@ -109,6 +110,7 @@
     table,
     near,
     far,
+    passing,
     planes,
     edge_l,
     edge_r,
@@ -120,6 +122,8 @@
     far_recv,
     halo_send,
     halo_recv,
+    pass_send,
+    pass_recv,
     local_sem,
 ):
     dates, n_rows, n_cols = sizes
@@ -193,6 +197,37 @@
             device_id=(mate, row, col),
             device_id_type=MESH,
         )
+
+    every = [(c, h) for c in order for h in range(pieces)]
+    direct = every[len(every) - DIRECT :]
+
+    def pass_copy(c, h):
+        n = direct.index((c, h))
+        return pltpu.make_async_remote_copy(
+            src_ref=img_hbm.at[:, :, band(c), pl.ds(h * PIECE, PIECE)],
+            dst_ref=passing.at[n],
+            send_sem=pass_send.at[n],
+            recv_sem=pass_recv.at[n],
+            device_id=(mate, row, col),
+            device_id_type=MESH,
+        )
+
+    def last_copy(c, h):
+        n = direct.index((c, h))
+        return pltpu.make_async_remote_copy(
+            src_ref=passing.at[n],
+            dst_ref=near.at[:, :, band(c), pl.ds(h * PIECE, PIECE)],
+            send_sem=pass_send.at[n],
+            recv_sem=near_recv.at[c * pieces + h],
+            device_id=(before, row, col),
+            device_id_type=MESH,
+        )
+
+    for c, h in direct:
+
+        @pl.when(jnp.logical_not(odd))
+        def _():
+            pass_copy(c, h).start()
 
     for c in order:
         for h in range(pieces):
@@ -306,16 +341,24 @@
             device_id_type=MESH,
         )
 
+    for c, h in direct:
+
+        @pl.when(odd)
+        def _():
+            pass_copy(c, h).wait_recv()
+            last_copy(c, h).start()
+
     load_img.wait()
-    every = [(c, h) for c in order for h in range(pieces)]
     summed = None
     for now, done in zip(every + [None], [None] + every):
         if now is not None:
             far_copy(*now).wait_recv()
 
-            @pl.when(jnp.logical_not(odd))
-            def _():
-                near_copy(*now, far).start()
+            if now not in direct:
+
+                @pl.when(jnp.logical_not(odd))
+                def _():
+                    near_copy(*now, far).start()
 
         if done is None:
             continue
@@ -464,7 +507,15 @@
     for c in range(chunks):
         for h in range(pieces):
             far_copy(c, h).wait_send()
+            if (c, h) not in direct:
+                near_copy(c, h, img_hbm).wait_send()
+    for c, h in direct:
+        pass_copy(c, h).wait_send()
+
+        @pl.when(odd)
+        def _():
             near_copy(c, h, img_hbm).wait_send()
+
     for step in steps:
 
         @pl.when(there(step))
@@ -510,6 +561,7 @@
             pltpu.VMEM(table.shape, jnp.bfloat16),
             pltpu.VMEM(images.shape, jnp.float32),
             pltpu.VMEM(images.shape, jnp.float32),
+            pltpu.VMEM((DIRECT,) + images.shape[:2] + (BAND, PIECE), jnp.float32),
             pltpu.VMEM((18, tall, LANES), jnp.float32),
             pltpu.VMEM((rows, LANES), jnp.float32),
             pltpu.VMEM((rows, LANES), jnp.float32),
@@ -521,6 +573,8 @@
             dma((chunks * (cols // PIECE),)),
             dma((6 + 2 * chunks,)),
             dma((6 + 2 * chunks,)),
+            dma((DIRECT,)),
+            dma((DIRECT,)),
             dma((3,)),
         ],
         compiler_params=pltpu.CompilerParams(

time: 27.5 us -> 27 us (0.982)
  Pallas kernels: 26.8 us -> 26.1 us
    pallas_call x1, Pallas kernels: 26 us -> 25.4 us  [body(): pl.pallas_call(functools.partial(kernel, sizes, starts), out_shape=(pltpu...]
where the time goes in v8:
time: 27 us; the launch traced here: 26.8 us
  Pallas kernels  26.1 us (97%)
  between operations  0.64 us (2%)
    pallas_call x1, Pallas kernels, body(): pl.pallas_call(functools.partial(kernel, sizes, starts), out_shape=(pltpu...  25.4 us
    pallas_call x1, Pallas kernels, body(): pl.pallas_call(write, out_shape=(out, out), in_specs=[vmem, vmem], out_sp...  0.73 us

profile of v8, /device:TPU:2, one launch (start us, length us, event | category | flops | bytes accessed | tf_op | source)
XLA Modules:
  0.0 26.8 jit_solution(849807144638519714)
XLA Ops:
  0.6 25.4 %shard_map.50 = (f32[2,3,2,24,96]{4,3,2,1,0:T(8,128)S(1)}, f32[2,3,2,24,96]{4,3,2,1,0:T(8,128)S(1)}) custom-call(s32[2,3]{1,0:T(2,128)} %sec_hbm.1, f32[2,2,48,768]{3,2,1,0:T(8,128)} %img_hbm.1, bf16[2,672,128]{2,1,0:T(8,128)(2,1)} %constant.2.clone.table_hbm), custom_call_target="tpu_custom_call" | custom-call | flops 1000000000 | bytes 1000000 | tf_op jit(solution)/shard_map/pallas_call | solution.py:553
  26.0 0.7 %shard_map.51 = (f32[2,3,2,24,96]{4,3,2,1,0:T(8,128)}, f32[2,3,2,24,96]{4,3,2,1,0:T(8,128)}) custom-call(f32[2,3,2,24,96]{4,3,2,1,0:T(8,128)S(1)} %get-tuple-element.4.filt_in, f32[2,3,2,24,96]{4,3,2,1,0:T(8,128)S(1)} %get-tuple-element.5.coh_in), custom_call_target="tpu_custom_call" | custom-call | tf_op jit(solution)/shard_map/pallas_call | solution.py:585

commit v9 on v8

--- a/solution.py
+++ b/solution.py
@@ -18,7 +18,7 @@
 LANES = 128
 BAND = 8
 PIECE = 256
-DIRECT = 2
+DIRECT = 1
 VMEM_BYTES = 64 * 1024 * 1024 - 800 * 1024
 MESH = pl.DeviceIdType.MESH
 

time: 27 us -> 27.4 us (1.015)
  Pallas kernels: 26.1 us -> 26.6 us
    pallas_call x1, Pallas kernels: 25.4 us -> 25.9 us  [body(): pl.pallas_call(functools.partial(kernel, sizes, starts), out_shape=(pltpu...]
where the time goes in v9:
time: 27.4 us; the launch traced here: 27.3 us
  Pallas kernels  26.6 us (97%)
  between operations  0.64 us (2%)
    pallas_call x1, Pallas kernels, body(): pl.pallas_call(functools.partial(kernel, sizes, starts), out_shape=(pltpu...  25.9 us
    pallas_call x1, Pallas kernels, body(): pl.pallas_call(write, out_shape=(out, out), in_specs=[vmem, vmem], out_sp...  0.73 us

profile of v9, /device:TPU:2, one launch (start us, length us, event | category | flops | bytes accessed | tf_op | source)
XLA Modules:
  0.0 27.3 jit_solution(12414745910383586202)
XLA Ops:
  0.6 25.9 %shard_map.50 = (f32[2,3,2,24,96]{4,3,2,1,0:T(8,128)S(1)}, f32[2,3,2,24,96]{4,3,2,1,0:T(8,128)S(1)}) custom-call(s32[2,3]{1,0:T(2,128)} %sec_hbm.1, f32[2,2,48,768]{3,2,1,0:T(8,128)} %img_hbm.1, bf16[2,672,128]{2,1,0:T(8,128)(2,1)} %constant.2.clone.table_hbm), custom_call_target="tpu_custom_call" | custom-call | flops 1000000000 | bytes 1000000 | tf_op jit(solution)/shard_map/pallas_call | solution.py:553
  26.5 0.7 %shard_map.51 = (f32[2,3,2,24,96]{4,3,2,1,0:T(8,128)}, f32[2,3,2,24,96]{4,3,2,1,0:T(8,128)}) custom-call(f32[2,3,2,24,96]{4,3,2,1,0:T(8,128)S(1)} %get-tuple-element.4.filt_in, f32[2,3,2,24,96]{4,3,2,1,0:T(8,128)S(1)} %get-tuple-element.5.coh_in), custom_call_target="tpu_custom_call" | custom-call | tf_op jit(solution)/shard_map/pallas_call | solution.py:585

commit v10 on v8

--- a/solution.py
+++ b/solution.py
@@ -351,18 +351,18 @@
     load_img.wait()
     summed = None
     for now, done in zip(every + [None], [None] + every):
-        if now is not None:
+        if now is not None and now not in direct:
             far_copy(*now).wait_recv()
 
-            if now not in direct:
-
-                @pl.when(jnp.logical_not(odd))
-                def _():
-                    near_copy(*now, far).start()
+            @pl.when(jnp.logical_not(odd))
+            def _():
+                near_copy(*now, far).start()
 
         if done is None:
             continue
         c, h = done
+        if done in direct:
+            far_copy(c, h).wait_recv()
         near_copy(c, h, img_hbm).wait_recv()
         part = look_sums(c, h)
         summed = part if h == 0 else summed + part

time: 27 us -> 27 us (level)
  no operation moved by 1% of the time
where the time goes in v10:
time: 27 us; the launch traced here: 26.8 us
  Pallas kernels  26.1 us (97%)
  between operations  0.64 us (2%)
    pallas_call x1, Pallas kernels, body(): pl.pallas_call(functools.partial(kernel, sizes, starts), out_shape=(pltpu...  25.4 us
    pallas_call x1, Pallas kernels, body(): pl.pallas_call(write, out_shape=(out, out), in_specs=[vmem, vmem], out_sp...  0.73 us

profile of v10, /device:TPU:2, one launch (start us, length us, event | category | flops | bytes accessed | tf_op | source)
XLA Modules:
  0.0 26.8 jit_solution(7065872279303296850)
XLA Ops:
  0.6 25.4 %shard_map.50 = (f32[2,3,2,24,96]{4,3,2,1,0:T(8,128)S(1)}, f32[2,3,2,24,96]{4,3,2,1,0:T(8,128)S(1)}) custom-call(s32[2,3]{1,0:T(2,128)} %sec_hbm.1, f32[2,2,48,768]{3,2,1,0:T(8,128)} %img_hbm.1, bf16[2,672,128]{2,1,0:T(8,128)(2,1)} %constant.2.clone.table_hbm), custom_call_target="tpu_custom_call" | custom-call | flops 1000000000 | bytes 1000000 | tf_op jit(solution)/shard_map/pallas_call | solution.py:553
  26.1 0.7 %shard_map.51 = (f32[2,3,2,24,96]{4,3,2,1,0:T(8,128)}, f32[2,3,2,24,96]{4,3,2,1,0:T(8,128)}) custom-call(f32[2,3,2,24,96]{4,3,2,1,0:T(8,128)S(1)} %get-tuple-element.4.filt_in, f32[2,3,2,24,96]{4,3,2,1,0:T(8,128)S(1)} %get-tuple-element.5.coh_in), custom_call_target="tpu_custom_call" | custom-call | tf_op jit(solution)/shard_map/pallas_call | solution.py:585
